TPU v7x, 512 devices: a whole 4x8x8 slice. The times are simulated.
512 devices in a mesh: sec: 128 (over z_hi, x, y, core), term: 4 (over z_lo).
Axes of the slice: x: 4, y: 8, z: 8 (z_hi: 2, z_lo: 4; z = z_hi * 4 + z_lo), core: 2. Of those that a mesh axis runs over, the one named last changes fastest.
Arguments:
- meet_env: bfloat16 [128, 24, 256, 256], P('sec', 'term'), may hold values from -0.375 to 0.375
- meet_iso: bfloat16 [128, 256, 2, 256], P('sec'), may hold values from -0.3125 to 0.3125
- last_site: bfloat16 [128, 256, 2, 256], P('sec'), may hold values from -60 to 60
- first_site: bfloat16 [128, 256, 2, 256], P('sec'), may hold values from -0.375 to 0.375
- term_kind: int32 [24, 2], P('term'), may hold values from 0 to 3
Outputs:
- two_site_out: float32 [128, 256, 2, 2, 256], P('sec')
All inputs are finite; a program needn't handle non-finite values.
Results may differ from a plain program's by a relative error of at most 0.013.
Values may be sent and summed in bfloat16 or wider, within the bound.
No kernel may reach another device: no remote copies, remote signals or barrier semaphores. Data moves between devices by JAX's collectives and lax.ppermute only.
A program may use at most 64 MiB of HBM per device.

v0:
```python
import jax
import jax.numpy as jnp
import numpy as np
from jax import lax
from jax.sharding import PartitionSpec as P

PHYS = 2
STEPS = 2


operator_table = np.array(
    [
        [[1.0, 0.0], [0.0, 1.0]],
        [[0.0, 1.0], [1.0, 0.0]],
        [[1.0, 0.0], [0.0, -1.0]],
        [[0.0, 1.0], [-1.0, 0.0]],
    ],
    dtype=np.float32,
)
step_size = 0.2
epsilon = 1e-06


def swapped(value, axis, bit):
    mask = 2**bit
    pairs = [(source, source ^ mask) for source in range(lax.axis_size(axis))]
    return lax.ppermute(value, axis, pairs)


def shifted(block, axis, distance):
    devices = range(lax.axis_size(axis))
    route = [((i - distance) % len(devices), i) for i in devices]
    return lax.ppermute(block, axis, route)


def joined_along(tiles, dim):
    shape = list(tiles.shape[1:])
    shape[dim] *= tiles.shape[0]
    return jnp.moveaxis(tiles, 0, dim).reshape(shape)


def copy_for_each(x, axis):
    copies = jnp.broadcast_to(x, (lax.axis_size(axis), *x.shape))
    return lax.all_to_all(copies, axis, split_axis=0, concat_axis=0, tiled=True)


def collect(x, axis, dim):
    return joined_along(copy_for_each(x, axis), dim)


def in_blocks(x, dim, size):
    before, after = (x.shape[:dim], x.shape[dim + 1 :])
    return jnp.moveaxis(x.reshape(*before, size, -1, *after), dim, 0)


def sent_and_summed(x, axis, dim):
    size = lax.axis_size(axis)
    tiles = lax.all_to_all(in_blocks(x, dim, size), axis, 0, 0, tiled=True)
    return jnp.sum(tiles.astype(jnp.float32), axis=0)


def over_copies(x, axis):
    return copy_for_each(x, axis).sum(axis=0)


def operator_pairs(term_kind):
    levels = jnp.arange(4, dtype=jnp.int32)
    onehot = (term_kind[:, :, None] == levels).astype(jnp.float32)
    return jnp.einsum("kjo,oxy->kjxy", onehot, jnp.asarray(operator_table, dtype=jnp.float32))


def reverse_bond(basis):
    return jnp.transpose(basis, (2, 1, 0))


def extend(environment, basis, operators):
    group_terms, bond_dim = (environment.shape[0], environment.shape[1])
    wide = jnp.dot(
        environment.reshape(group_terms * bond_dim, bond_dim),
        basis.reshape(bond_dim, 2 * bond_dim),
        preferred_element_type=jnp.float32,
    )
    wide = wide.astype(jnp.bfloat16).reshape(group_terms, bond_dim, 2, bond_dim)
    mixed = jnp.einsum(
        "kst,katm->kasm", operators.astype(jnp.bfloat16), wide, preferred_element_type=jnp.float32
    ).astype(jnp.bfloat16)
    return jnp.einsum("asm,kasn->kmn", basis, mixed, preferred_element_type=jnp.float32).astype(
        jnp.bfloat16
    )


def extend_twice(environment, first_basis, second_basis, operators):
    return extend(extend(environment, first_basis, operators), second_basis, operators)


def apply_local(vector, left_env, right_env, operators):
    pair_ops = jnp.einsum("ksx,kty->kstxy", operators[:, 0], operators[:, 1]).reshape(
        operators.shape[0], 4, 4
    )
    permuted = jnp.einsum(
        "kxy,ayc->kaxc", pair_ops.astype(jnp.bfloat16), vector, preferred_element_type=jnp.float32
    ).astype(jnp.bfloat16)
    left_applied = jnp.einsum(
        "kab,kbxc->kaxc", left_env, permuted, preferred_element_type=jnp.float32
    ).astype(jnp.bfloat16)
    return jnp.einsum("kaxc,kdc->axd", left_applied, right_env, preferred_element_type=jnp.float32)


def shards(meet_env, meet_iso, last_site, first_site, term_kind):
    own_env = meet_env[0]
    own_iso = meet_iso[0]
    own_last = last_site[0]
    own_first = first_site[0]
    bond_dim = own_env.shape[1]
    operators = operator_pairs(term_kind)
    odd_section = lax.axis_index("sec") % 2 == 1
    partner_env, partner_iso = swapped((own_env, own_iso), "sec", 0)
    first_basis = jnp.where(odd_section, partner_iso, reverse_bond(partner_iso))
    second_basis = jnp.where(odd_section, own_iso, reverse_bond(own_iso))
    chain_ops = jnp.where(odd_section, operators[:, 0], operators[:, 1])
    fresh_env = extend_twice(partner_env, first_basis, second_basis, chain_ops)
    came_env, came_site = shifted((fresh_env, own_last), "sec", 1)
    left_env = jnp.where(odd_section, partner_env, came_env)
    right_env = jnp.where(odd_section, own_env, fresh_env)
    two_site = jnp.dot(
        came_site.reshape(2 * bond_dim, bond_dim),
        own_first.reshape(bond_dim, 2 * bond_dim),
        preferred_element_type=jnp.float32,
    ).reshape(bond_dim, 4, bond_dim)
    share_rows = bond_dim // lax.axis_size("term")
    row_start = lax.axis_index("term") * share_rows
    row_share = lax.dynamic_slice_in_dim(two_site, row_start, share_rows, 0)
    vector = two_site.astype(jnp.bfloat16)
    for step_index in range(STEPS):
        if step_index > 0:
            vector = collect(row_share.astype(jnp.bfloat16), "term", 0)
        summed = sent_and_summed(
            apply_local(vector, left_env, right_env, operators).astype(jnp.bfloat16), "term", 0
        )
        row_share = row_share - step_size * summed
    share_total = over_copies(jnp.sum(row_share * row_share), "term")
    entry_count = float(two_site.size)
    scaled = row_share * lax.rsqrt(share_total / entry_count + epsilon)
    result = collect(scaled.astype(jnp.bfloat16), "term", 0).astype(scaled.dtype)
    return result.reshape(1, bond_dim, PHYS, PHYS, bond_dim)


def solution(mesh):
    in_specs = (
        P("sec", "term", None, None),
        P("sec", None, None, None),
        P("sec", None, None, None),
        P("sec", None, None, None),
        P("term", None),
    )
    out_specs = P("sec", None, None, None, None)
    return jax.shard_map(shards, mesh=mesh, in_specs=in_specs, out_specs=out_specs, check_vma=False)
```

profile of v0, /device:TPU:64, one launch (start us, length us, event | category | flops | bytes accessed | tf_op | source)
XLA Modules:
  0.0 149.1 jit_solution(12968061099169359223)
XLA Ops:
  0.0 1.3 copy.77
  1.4 2.1 %collective-permute-start.2 = (bf16[256,2,256]{0,1,2:T(2,128)(2,1)S(1)}, bf16[256,2,256]{0,1,2:T(2,128)(2,1)S(1)}, u32[]{:S(2)}, u32[]{:S(2)}) collective-permute-start(bf16[256,2,256]{0,1,2:T(2,128)(2,1)S(1)} %copy.77), channel_id=1, source_target_pairs={{0,4},{4,0},{8,12},{12,8},{16,20},{20,16},{24,28},{28,24},{32,36},... | collective-permute-start | bytes 786440 | tf_op jit(solution)/shard_map/ppermute | solution.py:27
  3.4 2.4 %collective-permute-start = (bf16[256,2,256]{2,1,0:T(2,128)(2,1)}, bf16[256,2,256]{2,1,0:T(2,128)(2,1)}, u32[]{:S(2)}, u32[]{:S(2)}) collective-permute-start(bf16[256,2,256]{2,1,0:T(2,128)(2,1)} %bitcast.138), channel_id=1, source_target_pairs={{508,0},{0,4},{4,8},{8,12},{12,16},{16,20},{20,24},{24,28},{28,32}... | collective-permute-start | bytes 786440 | tf_op jit(solution)/shard_map/ppermute | solution.py:33
  5.8 1.4 copy.76
  7.3 3.1 %collective-permute-start.1 = (bf16[6,256,256]{1,2,0:T(8,128)(2,1)S(1)}, bf16[6,256,256]{1,2,0:T(8,128)(2,1)}, u32[]{:S(2)}, u32[]{:S(2)}) collective-permute-start(bf16[6,256,256]{1,2,0:T(8,128)(2,1)S(1)} %bitcast.131), channel_id=1, source_target_pairs={{0,4},{4,0},{8,12},{12,8},{16,20},{20,16},{24,28},{28,24},{32,36},... | collective-permute-start | bytes 2359304 | tf_op jit(solution)/shard_map/ppermute | solution.py:27
  11.0 0.7 copy.126
  12.6 0.9 copy.83
  13.5 1.4 copy.79
  14.9 0.6 fusion.8
  15.5 0.7 copy.80
  16.7 1.8 %fusion.21 = bf16[6,256,2,256]{3,2,1,0:T(2,128)(2,1)S(1)} fusion(bf16[6,256,2,256]{3,2,1,0:T(2,128)(2,1)S(1)} %reshape.59, bf16[6,2,2,1]{2,1,3,0:T(2,128)(2,1)S(1)} %copy.102), kind=kOutput, calls=%fused_computation.21 | convolution fusion | flops 3932160 | bytes 3145776 | tf_op jit(solution)/shard_map/kst,katm->kasm/dot_general | solution.py:84
  18.5 0.6 bitcast_convert_fusion.1
  20.1 1.8 %fusion.22 = bf16[6,256,2,256]{3,2,1,0:T(2,128)(2,1)S(1)} fusion(bf16[6,256,2,256]{3,2,1,0:T(2,128)(2,1)S(1)} %reshape.62, bf16[6,2,2,1]{2,1,3,0:T(2,128)(2,1)S(1)} %copy.102), kind=kOutput, calls=%fused_computation.22 | convolution fusion | flops 3932160 | bytes 3145776 | tf_op jit(solution)/shard_map/kst,katm->kasm/dot_general | solution.py:84
  21.9 1.5 %fusion.37 = bf16[6,256,256]{1,2,0:T(8,128)(2,1)} fusion(bf16[6,256,2,256]{3,2,1,0:T(2,128)(2,1)S(1)} %fusion.22, bf16[256,2,256]{2,1,0:T(2,128)(2,1)S(1)} %copy-done.2), kind=kOutput, calls=%fused_computation.25 | convolution fusion | flops 403046400 | bytes 2621440 | tf_op jit(solution)/shard_map/asm,kasn->kmn/dot_general | solution.py:87
  23.4 2.1 %collective-permute-start.3 = (bf16[6,256,256]{1,2,0:T(8,128)(2,1)}, bf16[6,256,256]{1,2,0:T(8,128)(2,1)}, u32[]{:S(2)}, u32[]{:S(2)}) collective-permute-start(bf16[6,256,256]{1,2,0:T(8,128)(2,1)} %fusion.37), channel_id=1, source_target_pairs={{508,0},{0,4},{4,8},{8,12},{12,16},{16,20},{20,24},{24,28},{28,32}... | collective-permute-start | bytes 2359304 | tf_op jit(solution)/shard_map/ppermute | solution.py:33
  25.5 1.1 reshape.55
  27.2 3.2 %convert_bitcast_fusion.1 = bf16[6,256,4,256]{3,0,2,1:T(8,128)(2,1)} fusion(bf16[6,4,4,1]{0,2,1,3:T(4,128)(2,1)S(1)} %bitcast.136, bf16[256,4,256,1]{2,1,0,3:T(4,128)(2,1)S(1)} %reshape.75), kind=kOutput, calls=%fused_computation.1 | convolution fusion | flops 14155776 | bytes 3670208 | tf_op jit(solution)/shard_map/kxy,ayc->kaxc/dot_general | solution.py:100
  30.4 24.2 %collective-permute-done.3 = bf16[6,256,256]{1,2,0:T(8,128)(2,1)} collective-permute-done((bf16[6,256,256]{1,2,0:T(8,128)(2,1)}, bf16[6,256,256]{1,2,0:T(8,128)(2,1)}, u32[]{:S(2)}, u32[]{:S(2)}) %collective-permute-start.3) | collective-permute-done | bytes 786464 | tf_op jit(solution)/shard_map/ppermute | solution.py:33
  54.6 7.4 %fusion.45 = bf16[256,4,256]{2,0,1:T(8,128)(2,1)S(1)} fusion(bf16[6,256,4,256]{3,0,2,1:T(8,128)(2,1)} %convert_bitcast_fusion.1, bf16[6,256,256]{1,2,0:T(8,128)(2,1)} %collective-permute-done.1, bf16[6,256,256]{1,2,0:T(8,128)(2,1)} %collective-permute-done.3, pred[]{:T(512)S(6)} %eq.18, bf16[6,256,256]{1,2,0:T(8,128)(2,1)} %fusion.37, ...), kind=kOutput, calls=%fused_computation.27 | convolution fusion | flops 1613234176 | bytes 6815745 | tf_op jit(solution)/shard_map/kaxc,kdc->axd/dot_general | solution.py:106
  62.0 0.8 copy.91
  62.9 6.6 %all-to-all-start = ((bf16[4,64,4,256]{3,1,2,0:T(8,128)(2,1)}), bf16[4,64,4,256]{3,1,2,0:T(8,128)(2,1)S(1)}, u32[]{:S(2)}, u32[]{:S(2)}) async-start(bf16[4,64,4,256]{3,1,2,0:T(8,128)(2,1)} %copy.91), calls=%async_computation | async-start | bytes 1048576 | tf_op jit(solution)/shard_map/all_to_all | solution.py:58
  70.0 7.9 %all-to-all-done = bf16[4,64,4,256]{3,1,2,0:T(8,128)(2,1)S(1)} async-done(((bf16[4,64,4,256]{3,1,2,0:T(8,128)(2,1)}), bf16[4,64,4,256]{3,1,2,0:T(8,128)(2,1)S(1)}, u32[]{:S(2)}, u32[]{:S(2)}) %all-to-all-start) | async-done | bytes 524320 | tf_op jit(solution)/shard_map/all_to_all | solution.py:58
  78.4 17.1 %all_to_all.26 = bf16[4,64,4,256]{3,2,1,0:T(4,128)(2,1)S(1)} all-to-all(bf16[4,64,4,256]{3,2,1,0:T(4,128)(2,1)S(1)} %broadcast_in_dim.11), channel_id=1, replica_groups=mesh['sec'=128,'term'=4] {'term'}, dimensions={0} | all-to-all | bytes 1048576 | tf_op jit(solution)/shard_map/all_to_all | solution.py:44
  95.4 3.3 %convert_bitcast_fusion = bf16[6,256,4,256]{3,0,2,1:T(8,128)(2,1)} fusion(bf16[256,4,256,1]{2,1,3,0:T(4,128)(2,1)S(1)} %bitcast.125, bf16[6,4,4,1]{0,2,1,3:T(4,128)(2,1)S(1)} %bitcast.137), kind=kOutput, calls=%fused_computation | convolution fusion | flops 14155776 | bytes 3670208 | tf_op jit(solution)/shard_map/kxy,ayc->kaxc/dot_general | solution.py:100
  98.7 7.4 %fusion.40 = bf16[256,4,256]{2,0,1:T(8,128)(2,1)S(1)} fusion(bf16[6,256,4,256]{3,0,2,1:T(8,128)(2,1)} %convert_bitcast_fusion, bf16[6,256,256]{1,2,0:T(8,128)(2,1)} %collective-permute-done.1, bf16[6,256,256]{1,2,0:T(8,128)(2,1)} %collective-permute-done.3, pred[]{:T(512)S(6)} %eq.18, bf16[6,256,256]{1,2,0:T(8,128)(2,1)} %fusion.37, ...), kind=kOutput, calls=%fused_computation.26 | convolution fusion | flops 1613234176 | bytes 6815745 | tf_op jit(solution)/shard_map/kaxc,kdc->axd/dot_general | solution.py:106
  106.2 17.6 %all_to_all.27 = bf16[4,64,4,256]{3,1,2,0:T(8,128)(2,1)S(1)} all-to-all(bf16[4,64,4,256]{3,1,2,0:T(8,128)(2,1)S(1)} %copy.97), channel_id=1, replica_groups=mesh['sec'=128,'term'=4] {'term'}, dimensions={0} | all-to-all | bytes 1048576 | tf_op jit(solution)/shard_map/all_to_all | solution.py:58
  123.9 0.7 multiply_reduce_fusion
  124.5 0.6 broadcast_in_dim.12
  125.2 8.4 %all_to_all.28 = f32[4,1,1]{2,1,0:T(1,128)S(1)} all-to-all(f32[4,1,1]{2,1,0:T(1,128)S(1)} %broadcast_in_dim.12), channel_id=1, replica_groups=mesh['sec'=128,'term'=4] {'term'}, dimensions={0} | all-to-all | bytes 32 | tf_op jit(solution)/shard_map/all_to_all | solution.py:44
  133.6 0.6 reduce_sum.39
  135.3 12.3 %all_to_all.29 = bf16[4,64,4,256]{3,2,1,0:T(4,128)(2,1)S(1)} all-to-all(bf16[4,64,4,256]{3,2,1,0:T(4,128)(2,1)S(1)} %broadcast_in_dim.13), channel_id=1, replica_groups=mesh['sec'=128,'term'=4] {'term'}, dimensions={0} | all-to-all | bytes 1048576 | tf_op jit(solution)/shard_map/all_to_all | solution.py:44
  147.6 1.5 reshape.66
  (49 shorter events, 4.8 us)
Async XLA Ops:
  0.0 10.7 %copy-start.9 = (bf16[4,2,2,1]{0,2,1,3:T(2,128)(2,1)S(1)}, bf16[4,2,2,1]{0,2,1,3:T(2,128)(2,1)}, u32[]{:S(2)}) copy-start(bf16[4,2,2,1]{0,2,1,3:T(2,128)(2,1)} %constant.75) | copy-start | bytes 100
  0.0 10.4 %copy-start = (bf16[1,256,2,256]{3,2,1,0:T(2,128)(2,1)S(1)}, bf16[1,256,2,256]{3,2,1,0:T(2,128)(2,1)}, u32[]{:S(2)}) copy-start(bf16[1,256,2,256]{3,2,1,0:T(2,128)(2,1)} %param.7) | copy-start | bytes 786436
  0.0 10.7 %copy-start.8 = (s32[6,2]{0,1:T(2,128)S(1)}, s32[6,2]{0,1:T(2,128)}, u32[]{:S(2)}) copy-start(s32[6,2]{0,1:T(2,128)} %param.10) | copy-start | bytes 148
  1.4 9.6 %copy-start.6 = (bf16[1,256,2,256]{3,2,1,0:T(2,128)(2,1)S(1)}, bf16[1,256,2,256]{3,2,1,0:T(2,128)(2,1)}, u32[]{:S(2)}) copy-start(bf16[1,256,2,256]{3,2,1,0:T(2,128)(2,1)} %param.9) | copy-start | bytes 786436
  1.4 10.4 %collective-permute-start.2 = (bf16[256,2,256]{0,1,2:T(2,128)(2,1)S(1)}, bf16[256,2,256]{0,1,2:T(2,128)(2,1)S(1)}, u32[]{:S(2)}, u32[]{:S(2)}) collective-permute-start(bf16[256,2,256]{0,1,2:T(2,128)(2,1)S(1)} %copy.77), channel_id=1, source_target_pairs={{0,4},{4,0},{8,12},{12,8},{16,20},{20,16},{24,28},{28,24},{32,36},... | collective-permute-start | bytes 786440 | tf_op jit(solution)/shard_map/ppermute | solution.py:27
  3.4 22.1 %collective-permute-start = (bf16[256,2,256]{2,1,0:T(2,128)(2,1)}, bf16[256,2,256]{2,1,0:T(2,128)(2,1)}, u32[]{:S(2)}, u32[]{:S(2)}) collective-permute-start(bf16[256,2,256]{2,1,0:T(2,128)(2,1)} %bitcast.138), channel_id=1, source_target_pairs={{508,0},{0,4},{4,8},{8,12},{12,16},{16,20},{20,24},{24,28},{28,32}... | collective-permute-start | bytes 786440 | tf_op jit(solution)/shard_map/ppermute | solution.py:33
  7.3 5.3 %copy-start.4 = (bf16[1,6,256,256]{2,3,1,0:T(8,128)(2,1)}, bf16[1,6,256,256]{2,3,1,0:T(8,128)(2,1)S(1)}, u32[]{:S(2)}) copy-start(bf16[1,6,256,256]{2,3,1,0:T(8,128)(2,1)S(1)} %copy.76) | copy-start | bytes 2359300
  7.3 6.2 %collective-permute-start.1 = (bf16[6,256,256]{1,2,0:T(8,128)(2,1)S(1)}, bf16[6,256,256]{1,2,0:T(8,128)(2,1)}, u32[]{:S(2)}, u32[]{:S(2)}) collective-permute-start(bf16[6,256,256]{1,2,0:T(8,128)(2,1)S(1)} %bitcast.131), channel_id=1, source_target_pairs={{0,4},{4,0},{8,12},{12,8},{16,20},{20,16},{24,28},{28,24},{32,36},... | collective-permute-start | bytes 2359304 | tf_op jit(solution)/shard_map/ppermute | solution.py:27
  10.7 2.8 %copy-start.1 = (bf16[256,2,256]{2,1,0:T(2,128)(2,1)}, bf16[256,2,256]{2,1,0:T(2,128)(2,1)S(1)}, u32[]{:S(2)}) copy-start(bf16[256,2,256]{2,1,0:T(2,128)(2,1)S(1)} %broadcast_select_fusion.2) | copy-start | bytes 786436
  16.7 1.8 %copy-start.7 = (bf16[256,2,256]{0,2,1:T(8,128)(2,1)S(1)}, bf16[256,2,256]{0,2,1:T(8,128)(2,1)}, u32[]{:S(2)}) copy-start(bf16[256,2,256]{0,2,1:T(8,128)(2,1)} %copy.83) | copy-start | bytes 786436
  20.1 1.8 %copy-start.2 = (bf16[256,2,256]{2,1,0:T(2,128)(2,1)S(1)}, bf16[256,2,256]{2,1,0:T(2,128)(2,1)}, u32[]{:S(2)}) copy-start(bf16[256,2,256]{2,1,0:T(2,128)(2,1)} %copy-done.1) | copy-start | bytes 786436
  21.9 4.7 %copy-start.3 = (bf16[32,8,2,256]{3,1,2,0:T(8,128)(2,1)S(1)}, bf16[32,8,2,256]{3,1,2,0:T(8,128)(2,1)}, u32[]{:S(2)}) copy-start(bf16[32,8,2,256]{3,1,2,0:T(8,128)(2,1)} %copy.126) | copy-start | bytes 786436
  23.4 31.2 %collective-permute-start.3 = (bf16[6,256,256]{1,2,0:T(8,128)(2,1)}, bf16[6,256,256]{1,2,0:T(8,128)(2,1)}, u32[]{:S(2)}, u32[]{:S(2)}) collective-permute-start(bf16[6,256,256]{1,2,0:T(8,128)(2,1)} %fusion.37), channel_id=1, source_target_pairs={{508,0},{0,4},{4,8},{8,12},{12,16},{16,20},{20,24},{24,28},{28,32}... | collective-permute-start | bytes 2359304 | tf_op jit(solution)/shard_map/ppermute | solution.py:33
  27.2 27.4 %copy-start.5 = (bf16[1,6,256,256]{2,3,1,0:T(8,128)(2,1)S(1)}, bf16[1,6,256,256]{2,3,1,0:T(8,128)(2,1)}, u32[]{:S(2)}) copy-start(bf16[1,6,256,256]{2,3,1,0:T(8,128)(2,1)} %copy-done.4) | copy-start | bytes 2359300
  62.9 15.1 %all-to-all-start = ((bf16[4,64,4,256]{3,1,2,0:T(8,128)(2,1)}), bf16[4,64,4,256]{3,1,2,0:T(8,128)(2,1)S(1)}, u32[]{:S(2)}, u32[]{:S(2)}) async-start(bf16[4,64,4,256]{3,1,2,0:T(8,128)(2,1)} %copy.91), calls=%async_computation | async-start | bytes 1048576 | tf_op jit(solution)/shard_map/all_to_all | solution.py:58
where the time goes:
time: 150 us; the launch traced here: 149 us
  blocking collectives  55.5 us (37%)
  waiting for transfers between devices  32.1 us (21%)
  matrix products  28.5 us (19%)
  starting transfers between devices  16.3 us (11%)
  local copies, waits for them, and re-layouts  13.4 us (9%)
  other arithmetic  2.16 us (1%)
    all_to_all x3, blocking collectives, copy_for_each(): return lax.all_to_all(copies, axis, split_axis=0, concat_axis=0, tiled=True)  37.8 us
    ppermute x2, waiting for transfers between devices, shifted(): return lax.ppermute(block, axis, route)  24.2 us
    all_to_all x1, blocking collectives, sent_and_summed(): tiles = lax.all_to_all(in_blocks(x, dim, size), axis, 0, 0, tiled=True)  17.6 us
    dot_general x2, matrix products, apply_local(): jnp.einsum('kaxc,kdc->axd', left_applied, right_env, preferred_element_ty...  14.8 us
    all_to_all x1, waiting for transfers between devices, sent_and_summed(): tiles = lax.all_to_all(in_blocks(x, dim, size), axis, 0, 0, tiled=True)  7.93 us
    all_to_all x1, starting transfers between devices, sent_and_summed(): tiles = lax.all_to_all(in_blocks(x, dim, size), axis, 0, 0, tiled=True)  6.63 us
    dot_general x2, matrix products, apply_local(): jnp.einsum('kxy,ayc->kaxc', pair_ops.astype(jnp.bfloat16), vector, prefer...  6.48 us
    ppermute x2, starting transfers between devices, swapped(): return lax.ppermute(value, axis, pairs)  5.16 us
  transfers between devices with their start and end apart: 5, of which 2 were waited for; matrix products, arithmetic and copies ran while one was open for 13% of the time, Pallas kernels for 0%

commit v1 on v0

v1 whole, which is shorter than its diff:
```python
import functools

import jax
import jax.numpy as jnp
from jax import lax
from jax.experimental import pallas as pl
from jax.experimental.pallas import tpu as pltpu
from jax.sharding import PartitionSpec as P

STEP = 0.2
EPS = 1e-06
F32 = jnp.float32
BF16 = jnp.bfloat16

VMEM = pl.BlockSpec(memory_space=pltpu.VMEM)
SMEM = pl.BlockSpec(memory_space=pltpu.SMEM)


def nn(a, b):
    return lax.dot_general(a, b, (((1,), (0,)), ((), ())), preferred_element_type=F32)


def nt(a, b):
    return lax.dot_general(a, b, (((1,), (1,)), ((), ())), preferred_element_type=F32)


def identity(n):
    rows = lax.broadcasted_iota(jnp.int32, (n, n), 0)
    cols = lax.broadcasted_iota(jnp.int32, (n, n), 1)
    return (rows == cols).astype(F32).astype(BF16)


def call(body, out_shape, specs, scratch=(), flops=0, nbytes=0, aliases=None, mib=20):
    outs = out_shape if isinstance(out_shape, (tuple, list)) else (out_shape,)
    out_specs = [VMEM] * len(outs)
    return pl.pallas_call(
        body,
        out_shape=list(outs),
        in_specs=list(specs),
        out_specs=out_specs,
        scratch_shapes=list(scratch),
        input_output_aliases=aliases or {},
        compiler_params=pltpu.CompilerParams(vmem_limit_bytes=mib * 2**20),
        cost_estimate=pl.CostEstimate(flops=flops, bytes_accessed=nbytes, transcendentals=0),
    )


def extend(plain, kinds, env, iso, wide, out):
    terms, bond, _ = env.shape
    levels = [iso[s] for s in range(2)]
    if plain:
        eye = identity(bond)
        back = jnp.concatenate([nt(eye, level).astype(BF16) for level in levels], axis=1)
    else:
        back = jnp.concatenate(levels, axis=1)
    for k in range(terms):
        kind = kinds[0 if plain else 1, k]
        crossed = lax.rem(kind, 2) == 1
        lower = jnp.where(kind >= 2, -1.0, 1.0).astype(F32)
        value = env[k]
        left, right = [nn(value, level) if plain else nt(value, level) for level in levels]
        wide[k, :bond] = jnp.where(crossed, right, left).astype(BF16)
        wide[k, bond:] = (jnp.where(crossed, left, right) * lower).astype(BF16)
    for k in range(terms):
        out[k] = nn(back, wide[k]).astype(BF16)


def extend_first_body(place, kinds, env, iso, out, wide):
    for odd in range(2):

        @pl.when(place[0] == odd)
        def _():
            extend(odd == 0, kinds, env, iso, wide, out)


def extend_odd_body(place, kinds, env, iso, out, wide):
    @pl.when(place[0] == 1)
    def _():
        extend(True, kinds, env, iso, wide, out)


def extend_call(body, place, kinds, env, iso):
    terms, bond, _ = env.shape
    return call(
        body,
        jax.ShapeDtypeStruct(env.shape, BF16),
        [SMEM, SMEM, VMEM, VMEM],
        [pltpu.VMEM((terms, 2 * bond, bond), BF16)],
        flops=terms * 8 * bond**3,
        nbytes=4 * terms * bond * bond + 4 * bond * bond,
    )(place, kinds, env, iso)[0]


def store_right(kinds, k, vector, right, applied):
    bond = right.shape[0]
    kind0, kind1 = kinds[0, k], kinds[1, k]
    mask = 2 * lax.rem(kind0, 2) + lax.rem(kind1, 2)
    lower0 = jnp.where(kind0 >= 2, -1.0, 1.0).astype(F32)
    lower1 = jnp.where(kind1 >= 2, -1.0, 1.0).astype(F32)
    for y in range(4):
        part = nt(vector[y], right)
        x = y ^ mask
        sign = jnp.where(x >= 2, lower0, 1.0) * jnp.where(lax.rem(x, 2) == 1, lower1, 1.0)
        applied[x, k * bond : (k + 1) * bond, :] = (part * sign).astype(BF16)


def store_left(lefts, applied, out):
    size, _, rows, _ = out.shape
    joined = jnp.concatenate(lefts, axis=1)
    for x in range(4):
        part = nn(joined, applied[x]).astype(BF16)
        for q in range(size):
            out[q, x] = part[q * rows : (q + 1) * rows]


def first_body(place, kinds, last, first, own_env, partner_env, once, iso, *rest):
    applied, share, out, right_env, exact, vector, wide = rest
    terms, bond, _ = own_env.shape
    rows = share.shape[1]
    for s in range(2):
        before = jnp.where(place[0] == 1, partner_env[terms + s], last[s])
        for t in range(2):
            value = nn(before, first[t])
            exact[2 * s + t] = value
            vector[2 * s + t] = value.astype(BF16)
    start = pl.multiple_of(place[1] * rows, rows)
    for x in range(4):
        share[x] = exact[x, pl.ds(start, rows), :]

    @pl.when(place[0] == 1)
    def _():
        for k in range(terms):
            right = own_env[k]
            right_env[k] = right
            store_right(kinds, k, vector, right, applied)
        store_left([partner_env[k] for k in range(terms)], applied, out)

    @pl.when(place[0] == 0)
    def _():
        extend(False, kinds, once, iso, wide, right_env)
        for k in range(terms):
            store_right(kinds, k, vector, right_env[k], applied)


def first_call(size, place, kinds, last, first, own_env, partner_env, once, iso):
    terms, bond, _ = own_env.shape
    rows = bond // size
    return call(
        first_body,
        [
            jax.ShapeDtypeStruct((4, terms * bond, bond), BF16),
            jax.ShapeDtypeStruct((4, rows, bond), F32),
            jax.ShapeDtypeStruct((size, 4, rows, bond), BF16),
            jax.ShapeDtypeStruct(own_env.shape, BF16),
        ],
        [SMEM, SMEM] + [VMEM] * 6,
        [
            pltpu.VMEM((4, bond, bond), F32),
            pltpu.VMEM((4, bond, bond), BF16),
            pltpu.VMEM((terms, 2 * bond, bond), BF16),
        ],
        flops=(8 + 8 * terms) * bond**3,
        nbytes=(6 * terms + 8 * terms + 16) * bond * bond,
    )(place, kinds, last, first, own_env, partner_env, once, iso)


def second_body(count, place, applied, before, partner_env, *rest):
    pieces, relayed = rest[:count], rest[count:-2]
    out, left_env = rest[-2:]
    terms, bond, _ = left_env.shape

    @pl.when(place[0] == 0)
    def _():
        at = 0
        for n, piece in enumerate(pieces):
            rows = piece.shape[1]
            for k in range(terms):
                value = piece[k]
                if n > 0:
                    value = jnp.where(place[2] == 1, relayed[n - 1][k], value)
                left_env[k, at : at + rows, :] = value
            at += rows
        store_left([left_env[k] for k in range(terms)], applied, out)

    @pl.when(place[0] == 1)
    def _():
        for k in range(terms):
            left_env[k] = partner_env[k]
        for q in range(out.shape[0]):
            out[q] = before[q]


def second_call(place, applied, before, partner_env, pieces, relayed):
    terms, bond, _ = pieces[0].shape[0], before.shape[3], None
    return call(
        functools.partial(second_body, len(pieces)),
        [
            jax.ShapeDtypeStruct(before.shape, BF16),
            jax.ShapeDtypeStruct((terms, bond, bond), BF16),
        ],
        [SMEM] + [VMEM] * (3 + len(pieces) + len(relayed)),
        flops=8 * terms * bond**3,
        nbytes=12 * terms * bond * bond,
    )(place, applied, before, partner_env, *pieces, *relayed)


def apply_body(place, kinds, gathered, left_env, right_env, out, vector, applied):
    size, _, rows, bond = gathered.shape
    terms = left_env.shape[0]
    for q in range(size):
        for x in range(4):
            vector[x, q * rows : (q + 1) * rows, :] = gathered[q, x]
    for k in range(terms):
        store_right(kinds, k, vector, right_env[k], applied)
    store_left([left_env[k] for k in range(terms)], applied, out)


def apply_call(place, kinds, gathered, left_env, right_env):
    terms, bond, _ = left_env.shape
    return call(
        apply_body,
        jax.ShapeDtypeStruct(gathered.shape, BF16),
        [SMEM, SMEM] + [VMEM] * 3,
        [pltpu.VMEM((4, bond, bond), BF16), pltpu.VMEM((4, terms * bond, bond), BF16)],
        flops=16 * terms * bond**3,
        nbytes=8 * terms * bond * bond,
    )(place, kinds, gathered, left_env, right_env)[0]


def update_body(parts, share, new_share, rounded):
    size = parts.shape[0]
    for x in range(4):
        total = parts[0, x].astype(F32)
        for q in range(1, size):
            total = total + parts[q, x].astype(F32)
        value = share[x] - STEP * total
        new_share[x] = value
        rounded[x] = value.astype(BF16)


def update_call(parts, share):
    return call(
        update_body,
        [jax.ShapeDtypeStruct(share.shape, F32), jax.ShapeDtypeStruct(share.shape, BF16)],
        [VMEM, VMEM],
        flops=0,
        nbytes=4 * share.size * 4,
    )(parts, share)


def final_body(gathered, out):
    size, _, rows, bond = gathered.shape
    total = jnp.zeros((rows, bond), F32)
    for q in range(size):
        for x in range(4):
            value = gathered[q, x].astype(F32)
            total = total + value * value
    mean = jnp.sum(total) / (size * 4 * rows * bond)
    scale = lax.rsqrt(jnp.full((8, 128), mean + EPS, F32))[0:1, 0:1]
    halves = bond // 128
    pitch = 4 * halves
    for q in range(size):
        for x in range(4):
            value = gathered[q, x].astype(F32) * scale
            s, t = x // 2, x % 2
            for j in range(halves):
                begin = q * rows * pitch + s * 2 * halves + j * 2 + t
                out[pl.ds(begin, rows, stride=pitch), :] = value[:, j * 128 : (j + 1) * 128]


def final_call(gathered):
    size, _, rows, bond = gathered.shape
    halves = bond // 128
    flat = call(
        final_body,
        jax.ShapeDtypeStruct((size * rows * 4 * halves, 128), F32),
        [VMEM],
        nbytes=gathered.size * 6,
    )(gathered)[0]
    blocks = flat.reshape(size * rows, 2, halves, 2, 128)
    return jnp.transpose(blocks, (0, 1, 3, 2, 4)).reshape(1, size * rows, 2, 2, bond)


def levels_first(site):
    return jnp.transpose(site, (1, 0, 2))


def shards(meet_env, meet_iso, last_site, first_site, term_kind):
    sections, size = lax.axis_size("sec"), lax.axis_size("term")
    both = ("sec", "term")
    own_env = meet_env[0]
    section = lax.axis_index("sec")
    half = sections // 2
    far = (section % half == 0).astype(jnp.int32)
    place = jnp.stack([section % 2, lax.axis_index("term"), far]).astype(jnp.int32)
    kinds = term_kind.T
    bond = own_env.shape[1]

    swap = [(i, i ^ 1) for i in range(sections)]
    to_odd = [(i, i + 1) for i in range(0, sections, 2)]
    to_even = [(i, (i + 1) % sections) for i in range(1, sections, 2)]
    ends = [half - 1, sections - 1]

    def pairs(steps):
        return [(i % sections * size + z, j % sections * size + z) for i, j in steps for z in range(size)]

    near = [(i, j) for i, j in to_even if i not in ends]
    z_first = near + [(i, i + half) for i in ends]
    then_xy = [(i + half, i + 1) for i in ends]

    own_iso = levels_first(meet_iso[0])
    own_last = levels_first(last_site[0])
    once = extend_call(extend_first_body, place, kinds, own_env, own_iso)
    own_last, _ = lax.optimization_barrier((own_last, once))
    once = lax.ppermute(once, "sec", swap)
    came_last = lax.ppermute(own_last, "sec", to_even)
    fresh = extend_call(extend_odd_body, place, kinds, once, own_iso)
    bundle, fresh = lax.optimization_barrier((jnp.concatenate([own_env, own_last]), fresh))
    cut = bond * 5 // 8
    z_piece = lax.ppermute(fresh[:, cut:], both, pairs(z_first))
    direct = lax.ppermute(fresh[:, :cut], both, pairs(to_even))
    partner_env = lax.ppermute(bundle, "sec", to_odd)
    z_piece, came_last = lax.optimization_barrier((z_piece, came_last))
    relayed = lax.ppermute(z_piece, both, pairs(then_xy))
    first = levels_first(first_site[0])
    applied, share, summand, right_env = first_call(
        size, place, kinds, came_last, first, own_env, partner_env, once, own_iso
    )
    summand, left_env = second_call(
        place, applied, summand, partner_env, [direct, z_piece], [relayed]
    )
    parts = lax.all_to_all(summand, "term", 0, 0, tiled=True)
    share, rounded = update_call(parts, share)
    gathered = lax.all_gather(rounded, "term")
    summand = apply_call(place, kinds, gathered, left_env, right_env)
    parts = lax.all_to_all(summand, "term", 0, 0, tiled=True)
    share, rounded = update_call(parts, share)
    gathered = lax.all_gather(rounded, "term")
    return final_call(gathered)


def solution(mesh):
    in_specs = (
        P("sec", "term", None, None),
        P("sec", None, None, None),
        P("sec", None, None, None),
        P("sec", None, None, None),
        P("term", None),
    )
    out_specs = P("sec", None, None, None, None)
    return jax.shard_map(shards, mesh=mesh, in_specs=in_specs, out_specs=out_specs, check_vma=False)
```

time: 150 us -> 112 us (0.75)
  the two profiles are of different devices: /device:TPU:64 before, /device:TPU:256 now
where the time goes in v1:
time: 112 us; the launch traced here: 111 us
  blocking collectives  59.2 us (53%)
  waiting for transfers between devices  27.9 us (25%)
  Pallas kernels  11.3 us (10%)
  starting transfers between devices  9.67 us (9%)
  local copies, waits for them, and re-layouts  2.97 us (3%)
    all_gather x2, blocking collectives, shards(): gathered = lax.all_gather(rounded, 'term')  30.3 us
    all_to_all x2, blocking collectives, shards(): parts = lax.all_to_all(summand, 'term', 0, 0, tiled=True)  28.9 us
    ppermute x1, waiting for transfers between devices, shards(): came_last = lax.ppermute(own_last, 'sec', to_even)  17.2 us
    ppermute x1, waiting for transfers between devices, shards(): direct = lax.ppermute(fresh[:, :cut], both, pairs(to_even))  6.13 us
    ppermute x1, starting transfers between devices, shards(): partner_env = lax.ppermute(bundle, 'sec', to_odd)  3.2 us
    unnamed x15, local copies, waits for them, and re-layouts  2.91 us
    pallas_call x1, Pallas kernels, first_call(): call(first_body, [jax.ShapeDtypeStruct((4, terms * bond, bond), BF16), ja...  2.75 us
    pallas_call x1, Pallas kernels, apply_call(): call(apply_body, jax.ShapeDtypeStruct(gathered.shape, BF16), [SMEM, SMEM]...  2.59 us
  transfers between devices with their start and end apart: 6, of which 4 were waited for; matrix products, arithmetic and copies ran while one was open for 0% of the time, Pallas kernels for 2%

profile of v1, /device:TPU:256, one launch (start us, length us, event | category | flops | bytes accessed | tf_op | source)
XLA Modules:
  0.0 111.4 jit_solution(13671954153629792598)
XLA Ops:
  0.0 1.0 copy.18
  1.0 0.1 pad_add_fusion.place
  1.1 1.1 %copy-done = bf16[1,6,256,256]{3,2,1,0:T(8,128)(2,1)S(1)} copy-done((bf16[1,6,256,256]{3,2,1,0:T(8,128)(2,1)S(1)}, bf16[1,6,256,256]{3,2,1,0:T(8,128)(2,1)}, u32[]{:S(2)}) %copy-start) | copy-done | bytes 786456
  2.3 0.7 copy-done.2
  2.9 1.7 %shard_map.55 = bf16[6,256,256]{2,1,0:T(8,128)(2,1)S(1)} custom-call(s32[3]{0:T(128)S(1)} %pad_add_fusion.place, s32[2,6]{1,0:T(2,128)S(1)} %bitcast.36, bf16[6,256,256]{2,1,0:T(8,128)(2,1)S(1)} %bitcast.28, bf16[2,256,256]{2,1,0:T(8,128)(2,1)S(1)} %bitcast.32), custom_call_target="tpu_custom_call" | custom-call | flops 805306368 | bytes 1835008 | tf_op jit(solution)/shard_map/pallas_call | solution.py:84
  4.6 1.9 %collective-permute-start = (bf16[6,256,256]{2,1,0:T(8,128)(2,1)S(1)}, bf16[6,256,256]{2,1,0:T(8,128)(2,1)S(1)}, u32[]{:S(2)}, u32[]{:S(2)}) collective-permute-start(bf16[6,256,256]{2,1,0:T(8,128)(2,1)S(1)} %shard_map.55), channel_id=1, source_target_pairs={{0,4},{4,0},{8,12},{12,8},{16,20},{20,16},{24,28},{28,24},{32,36},... | collective-permute-start | bytes 2359304 | tf_op jit(solution)/shard_map/ppermute | solution.py:315
  6.6 0.0 copy-start.5
  6.6 0.0 copy-start.1
  6.6 0.1 pad_maximum_fusion
  6.7 2.1 %collective-permute-done.env.once = bf16[6,256,256]{2,1,0:T(8,128)(2,1)S(1)} collective-permute-done((bf16[6,256,256]{2,1,0:T(8,128)(2,1)S(1)}, bf16[6,256,256]{2,1,0:T(8,128)(2,1)S(1)}, u32[]{:S(2)}, u32[]{:S(2)}) %collective-permute-start) | collective-permute-done | bytes 786464 | tf_op jit(solution)/shard_map/ppermute | solution.py:315
  8.8 0.6 shard_map.56
  9.3 3.2 %collective-permute-start.3 = (bf16[8,256,256]{2,1,0:T(8,128)(2,1)S(1)}, bf16[8,256,256]{2,1,0:T(8,128)(2,1)S(1)}, u32[]{:S(2)}, u32[]{:S(2)}) collective-permute-start(bf16[8,256,256]{2,1,0:T(8,128)(2,1)S(1)} %pad_maximum_fusion), channel_id=1, source_target_pairs={{0,4},{8,12},{16,20},{24,28},{32,36},{40,44},{48,52},{56,60},{64,6... | collective-permute-start | bytes 3145736 | tf_op jit(solution)/shard_map/ppermute | solution.py:322
  12.6 0.7 collective-permute-start.1
  13.3 1.3 %collective-permute-start.2 = (bf16[2,256,256]{2,1,0:T(8,128)(2,1)S(1)}, bf16[2,256,256]{2,1,0:T(8,128)(2,1)S(1)}, u32[]{:S(2)}, u32[]{:S(2)}) collective-permute-start(bf16[2,256,256]{2,1,0:T(8,128)(2,1)S(1)} %bitcast.41), channel_id=1, source_target_pairs={{4,8},{12,16},{20,24},{28,32},{36,40},{44,48},{52,56},{60,64},{68,... | collective-permute-start | bytes 786440 | tf_op jit(solution)/shard_map/ppermute | solution.py:316
  14.6 1.3 %collective-permute-start.4 = (bf16[6,160,256]{2,1,0:T(8,128)(2,1)S(1)}, bf16[6,160,256]{2,1,0:T(8,128)(2,1)S(1)}, u32[]{:S(2)}, u32[]{:S(2)}) collective-permute-start(bf16[6,160,256]{2,1,0:T(8,128)(2,1)S(1)} %slice.7), channel_id=1, source_target_pairs={{4,8},{5,9},{6,10},{7,11},{12,16},{13,17},{14,18},{15,19},{20,24},... | collective-permute-start | bytes 1474568 | tf_op jit(solution)/shard_map/ppermute | solution.py:321
  15.9 17.2 %collective-permute-done.2.last = bf16[2,256,256]{2,1,0:T(8,128)(2,1)S(1)} collective-permute-done((bf16[2,256,256]{2,1,0:T(8,128)(2,1)S(1)}, bf16[2,256,256]{2,1,0:T(8,128)(2,1)S(1)}, u32[]{:S(2)}, u32[]{:S(2)}) %collective-permute-start.2) | collective-permute-done | bytes 262176 | tf_op jit(solution)/shard_map/ppermute | solution.py:316
  33.1 0.0 collective-permute-done.1.rest_1_
  33.1 1.3 %collective-permute-start.5 = (bf16[6,96,256]{2,1,0:T(8,128)(2,1)S(1)}, bf16[6,96,256]{2,1,0:T(8,128)(2,1)S(1)}, u32[]{:S(2)}, u32[]{:S(2)}) collective-permute-start(bf16[6,96,256]{2,1,0:T(8,128)(2,1)S(1)} %collective-permute-done.1.rest_1_), channel_id=1, source_target_pairs={{508,256},{509,257},{510,258},{511,259},{252,0},{253,1},{254,2},{2... | collective-permute-start | bytes 884744 | tf_op jit(solution)/shard_map/ppermute | solution.py:324
  34.4 0.0 collective-permute-done.3.partner_env
  34.4 2.7 %shard_map.57 = (bf16[4,1536,256]{2,1,0:T(8,128)(2,1)S(1)}, f32[4,64,256]{2,1,0:T(8,128)S(1)}, bf16[4,4,64,256]{3,2,1,0:T(8,128)(2,1)S(1)}, bf16[6,256,256]{2,1,0:T(8,128)(2,1)S(1)}) custom-call(s32[3]{0:T(128)S(1)} %pad_add_fusion.place, s32[2,6]{1,0:T(2,128)S(1)} %bitcast.38, bf16[2,256,256]{2,1,0:T(8,128)(2,1)S(1)} %collective-permute-done.2.last, ...), custom_call_target="tpu_custom_call" | custom-call | flops 939524096 | bytes 6553600 | tf_op jit(solution)/shard_map/pallas_call | solution.py:148
  37.2 6.1 %collective-permute-done.4.rest_0_ = bf16[6,160,256]{2,1,0:T(8,128)(2,1)S(1)} collective-permute-done((bf16[6,160,256]{2,1,0:T(8,128)(2,1)S(1)}, bf16[6,160,256]{2,1,0:T(8,128)(2,1)S(1)}, u32[]{:S(2)}, u32[]{:S(2)}) %collective-permute-start.4) | collective-permute-done | bytes 491552 | tf_op jit(solution)/shard_map/ppermute | solution.py:321
  43.3 2.5 %collective-permute-done.5.rest_2_ = bf16[6,96,256]{2,1,0:T(8,128)(2,1)S(1)} collective-permute-done((bf16[6,96,256]{2,1,0:T(8,128)(2,1)S(1)}, bf16[6,96,256]{2,1,0:T(8,128)(2,1)S(1)}, u32[]{:S(2)}, u32[]{:S(2)}) %collective-permute-start.5) | collective-permute-done | bytes 294944 | tf_op jit(solution)/shard_map/ppermute | solution.py:324
  45.8 1.5 %shard_map.58 = (bf16[4,4,64,256]{3,2,1,0:T(8,128)(2,1)S(1)}, bf16[6,256,256]{2,1,0:T(8,128)(2,1)S(1)}) custom-call(s32[3]{0:T(128)S(1)} %pad_add_fusion.place, bf16[4,1536,256]{2,1,0:T(8,128)(2,1)S(1)} %get-tuple-element.23.applied, bf16[4,4,64,256]{3,2,1,0:T(8,128)(2,1)S(1)} %get-tuple-element.24.before, ...), custom_call_target="tpu_custom_call" | custom-call | flops 805306368 | bytes 4718592 | tf_op jit(solution)/shard_map/pallas_call | solution.py:195
  47.3 16.2 %all_to_all.10.parts = bf16[4,4,64,256]{3,2,1,0:T(8,128)(2,1)S(1)} all-to-all(bf16[4,4,64,256]{3,2,1,0:T(8,128)(2,1)S(1)} %get-tuple-element.26), channel_id=1, replica_groups=mesh['sec'=128,'term'=4] {'term'}, dimensions={0} | all-to-all | bytes 1048576 | tf_op jit(solution)/shard_map/all_to_all | solution.py:332
  63.5 0.1 shard_map.59
  63.6 15.7 %all-gather = bf16[16,64,256]{2,1,0:T(8,128)(2,1)S(1)} all-gather(bf16[4,64,256]{2,1,0:T(8,128)(2,1)S(1)} %get-tuple-element.28), channel_id=2, replica_groups=mesh['sec'=128,'term'=4] {'term'}, dimensions={0}, use_global_device_ids=true | all-gather | bytes 655360 | tf_op jit(solution)/shard_map/all_gather | solution.py:334
  79.3 0.0 copy-done.3
  79.3 2.6 %shard_map.60 = bf16[4,4,64,256]{3,2,1,0:T(8,128)(2,1)S(1)} custom-call(s32[3]{0:T(128)S(1)} %pad_add_fusion.place, s32[2,6]{1,0:T(2,128)S(1)} %bitcast.39, bf16[4,4,64,256]{3,2,1,0:T(8,128)(2,1)S(1)} %bitcast.31, bf16[6,256,256]{2,1,0:T(8,128)(2,1)S(1)} %get-tuple-element.29.left_env, bf16[6,256,256]{2,1,0:T(8,128)(2,1)S(1)} %get-tuple-element.30.right_env), custom_call_target="tpu_custom_call" | custom-call | flops 1610612736 | bytes 3145728 | tf_op jit(solution)/shard_map/pallas_call | solution.py:220
  81.9 12.7 %all_to_all.11.parts = bf16[4,4,64,256]{3,2,1,0:T(8,128)(2,1)S(1)} all-to-all(bf16[4,4,64,256]{3,2,1,0:T(8,128)(2,1)S(1)} %shard_map.60), channel_id=1, replica_groups=mesh['sec'=128,'term'=4] {'term'}, dimensions={0} | all-to-all | bytes 1048576 | tf_op jit(solution)/shard_map/all_to_all | solution.py:336
  94.6 0.8 shard_map.61
  95.4 14.6 %all-gather.1 = bf16[16,64,256]{2,1,0:T(8,128)(2,1)S(1)} all-gather(bf16[4,64,256]{2,1,0:T(8,128)(2,1)S(1)} %get-tuple-element.32), channel_id=3, replica_groups=mesh['sec'=128,'term'=4] {'term'}, dimensions={0}, use_global_device_ids=true | all-gather | bytes 655360 | tf_op jit(solution)/shard_map/all_gather | solution.py:338
  110.0 1.3 %shard_map.62 = f32[2048,128]{1,0:T(8,128)} custom-call(bf16[4,4,64,256]{3,2,1,0:T(8,128)(2,1)S(1)} %bitcast.27), custom_call_target="tpu_custom_call" | custom-call | bytes 1572864 | tf_op jit(solution)/shard_map/pallas_call | solution.py:274
  (11 shorter events, 0.1 us)
Async XLA Ops:
  0.0 6.5 %copy-start.4 = (bf16[1,256,2,256]{3,2,1,0:T(2,128)(2,1)S(1)}, bf16[1,256,2,256]{3,2,1,0:T(2,128)(2,1)}, u32[]{:S(2)}) copy-start(bf16[1,256,2,256]{3,2,1,0:T(2,128)(2,1)} %param.7) | copy-start | bytes 786436
  1.1 1.1 %copy-start = (bf16[1,6,256,256]{3,2,1,0:T(8,128)(2,1)S(1)}, bf16[1,6,256,256]{3,2,1,0:T(8,128)(2,1)}, u32[]{:S(2)}) copy-start(bf16[1,6,256,256]{3,2,1,0:T(8,128)(2,1)} %param.5) | copy-start | bytes 2359300
  2.2 0.7 copy-start.2
  4.6 4.2 %collective-permute-start = (bf16[6,256,256]{2,1,0:T(8,128)(2,1)S(1)}, bf16[6,256,256]{2,1,0:T(8,128)(2,1)S(1)}, u32[]{:S(2)}, u32[]{:S(2)}) collective-permute-start(bf16[6,256,256]{2,1,0:T(8,128)(2,1)S(1)} %shard_map.55), channel_id=1, source_target_pairs={{0,4},{4,0},{8,12},{12,8},{16,20},{20,16},{24,28},{28,24},{32,36},... | collective-permute-start | bytes 2359304 | tf_op jit(solution)/shard_map/ppermute | solution.py:315
  6.6 27.8 %copy-start.5 = (bf16[1,256,2,256]{3,2,1,0:T(2,128)(2,1)S(1)}, bf16[1,256,2,256]{3,2,1,0:T(2,128)(2,1)}, u32[]{:S(2)}) copy-start(bf16[1,256,2,256]{3,2,1,0:T(2,128)(2,1)} %param.8) | copy-start | bytes 786436
  6.6 27.9 %copy-start.1 = (bf16[1,6,256,256]{3,2,1,0:T(8,128)(2,1)S(1)}, bf16[1,6,256,256]{3,2,1,0:T(8,128)(2,1)}, u32[]{:S(2)}) copy-start(bf16[1,6,256,256]{3,2,1,0:T(8,128)(2,1)} %param.5) | copy-start | bytes 2359300
  9.3 25.1 %collective-permute-start.3 = (bf16[8,256,256]{2,1,0:T(8,128)(2,1)S(1)}, bf16[8,256,256]{2,1,0:T(8,128)(2,1)S(1)}, u32[]{:S(2)}, u32[]{:S(2)}) collective-permute-start(bf16[8,256,256]{2,1,0:T(8,128)(2,1)S(1)} %pad_maximum_fusion), channel_id=1, source_target_pairs={{0,4},{8,12},{16,20},{24,28},{32,36},{40,44},{48,52},{56,60},{64,6... | collective-permute-start | bytes 3145736 | tf_op jit(solution)/shard_map/ppermute | solution.py:322
  12.6 20.5 %collective-permute-start.1 = (bf16[6,96,256]{2,1,0:T(8,128)(2,1)S(1)}, bf16[6,96,256]{2,1,0:T(8,128)(2,1)S(1)}, u32[]{:S(2)}, u32[]{:S(2)}) collective-permute-start(bf16[6,96,256]{2,1,0:T(8,128)(2,1)S(1)} %slice.6), channel_id=1, source_target_pairs={{4,8},{5,9},{6,10},{7,11},{12,16},{13,17},{14,18},{15,19},{20,24},... | collective-permute-start | bytes 884744 | tf_op jit(solution)/shard_map/ppermute | solution.py:320
  13.3 19.8 %collective-permute-start.2 = (bf16[2,256,256]{2,1,0:T(8,128)(2,1)S(1)}, bf16[2,256,256]{2,1,0:T(8,128)(2,1)S(1)}, u32[]{:S(2)}, u32[]{:S(2)}) collective-permute-start(bf16[2,256,256]{2,1,0:T(8,128)(2,1)S(1)} %bitcast.41), channel_id=1, source_target_pairs={{4,8},{12,16},{20,24},{28,32},{36,40},{44,48},{52,56},{60,64},{68,... | collective-permute-start | bytes 786440 | tf_op jit(solution)/shard_map/ppermute | solution.py:316
  14.6 28.7 %collective-permute-start.4 = (bf16[6,160,256]{2,1,0:T(8,128)(2,1)S(1)}, bf16[6,160,256]{2,1,0:T(8,128)(2,1)S(1)}, u32[]{:S(2)}, u32[]{:S(2)}) collective-permute-start(bf16[6,160,256]{2,1,0:T(8,128)(2,1)S(1)} %slice.7), channel_id=1, source_target_pairs={{4,8},{5,9},{6,10},{7,11},{12,16},{13,17},{14,18},{15,19},{20,24},... | collective-permute-start | bytes 1474568 | tf_op jit(solution)/shard_map/ppermute | solution.py:321
  33.1 12.7 %collective-permute-start.5 = (bf16[6,96,256]{2,1,0:T(8,128)(2,1)S(1)}, bf16[6,96,256]{2,1,0:T(8,128)(2,1)S(1)}, u32[]{:S(2)}, u32[]{:S(2)}) collective-permute-start(bf16[6,96,256]{2,1,0:T(8,128)(2,1)S(1)} %collective-permute-done.1.rest_1_), channel_id=1, source_target_pairs={{508,256},{509,257},{510,258},{511,259},{252,0},{253,1},{254,2},{2... | collective-permute-start | bytes 884744 | tf_op jit(solution)/shard_map/ppermute | solution.py:324
  45.8 33.5 %copy-start.3 = (s32[6,2]{0,1:T(2,128)S(1)}, s32[6,2]{0,1:T(2,128)}, u32[]{:S(2)}) copy-start(s32[6,2]{0,1:T(2,128)} %param.9) | copy-start | bytes 148

commit v2 on v1

--- a/solution.py
+++ b/solution.py
@@ -227,25 +227,9 @@
     )(place, kinds, gathered, left_env, right_env)[0]
 
 
-def update_body(parts, share, new_share, rounded):
-    size = parts.shape[0]
-    for x in range(4):
-        total = parts[0, x].astype(F32)
-        for q in range(1, size):
-            total = total + parts[q, x].astype(F32)
-        value = share[x] - STEP * total
-        new_share[x] = value
-        rounded[x] = value.astype(BF16)
-
-
-def update_call(parts, share):
-    return call(
-        update_body,
-        [jax.ShapeDtypeStruct(share.shape, F32), jax.ShapeDtypeStruct(share.shape, BF16)],
-        [VMEM, VMEM],
-        flops=0,
-        nbytes=4 * share.size * 4,
-    )(parts, share)
+def update(parts, share):
+    share = share - STEP * jnp.sum(parts.astype(F32), axis=0)
+    return share, share.astype(BF16)
 
 
 def final_body(gathered, out):
@@ -330,11 +314,11 @@
         place, applied, summand, partner_env, [direct, z_piece], [relayed]
     )
     parts = lax.all_to_all(summand, "term", 0, 0, tiled=True)
-    share, rounded = update_call(parts, share)
+    share, rounded = update(parts, share)
     gathered = lax.all_gather(rounded, "term")
     summand = apply_call(place, kinds, gathered, left_env, right_env)
     parts = lax.all_to_all(summand, "term", 0, 0, tiled=True)
-    share, rounded = update_call(parts, share)
+    share, rounded = update(parts, share)
     gathered = lax.all_gather(rounded, "term")
     return final_call(gathered)
 

time: 112 us -> 112 us (level)
    unnamed x15 -> x13, local copies, waits for them, and re-layouts: 2.91 us -> 2.91 us
where the time goes in v2:
time: 112 us; the launch traced here: 111 us
  blocking collectives  59.6 us (53%)
  waiting for transfers between devices  27.9 us (25%)
  Pallas kernels  10.4 us (9%)
  starting transfers between devices  9.67 us (9%)
  local copies, waits for them, and re-layouts  2.96 us (3%)
    all_gather x2, blocking collectives, shards(): gathered = lax.all_gather(rounded, 'term')  30.8 us
    all_to_all x2, blocking collectives, shards(): parts = lax.all_to_all(summand, 'term', 0, 0, tiled=True)  28.8 us
    ppermute x1, waiting for transfers between devices, shards(): came_last = lax.ppermute(own_last, 'sec', to_even)  17.2 us
    ppermute x1, waiting for transfers between devices, shards(): direct = lax.ppermute(fresh[:, :cut], both, pairs(to_even))  6.13 us
    ppermute x1, starting transfers between devices, shards(): partner_env = lax.ppermute(bundle, 'sec', to_odd)  3.2 us
    unnamed x13, local copies, waits for them, and re-layouts  2.91 us
    pallas_call x1, Pallas kernels, first_call(): call(first_body, [jax.ShapeDtypeStruct((4, terms * bond, bond), BF16), ja...  2.75 us
    pallas_call x1, Pallas kernels, apply_call(): call(apply_body, jax.ShapeDtypeStruct(gathered.shape, BF16), [SMEM, SMEM]...  2.6 us
  transfers between devices with their start and end apart: 6, of which 4 were waited for; matrix products, arithmetic and copies ran while one was open for 0% of the time, Pallas kernels for 2%

profile of v2, /device:TPU:256, one launch (start us, length us, event | category | flops | bytes accessed | tf_op | source)
XLA Modules:
  0.0 111.2 jit_solution(11267015938164568985)
XLA Ops:
  0.0 1.0 copy.18
  1.0 0.1 pad_add_fusion.place
  1.1 1.1 %copy-done = bf16[1,6,256,256]{3,2,1,0:T(8,128)(2,1)S(1)} copy-done((bf16[1,6,256,256]{3,2,1,0:T(8,128)(2,1)S(1)}, bf16[1,6,256,256]{3,2,1,0:T(8,128)(2,1)}, u32[]{:S(2)}) %copy-start) | copy-done | bytes 786456
  2.3 0.7 copy-done.2
  2.9 1.7 %shard_map.55 = bf16[6,256,256]{2,1,0:T(8,128)(2,1)S(1)} custom-call(s32[3]{0:T(128)S(1)} %pad_add_fusion.place, s32[2,6]{1,0:T(2,128)S(1)} %bitcast.36, bf16[6,256,256]{2,1,0:T(8,128)(2,1)S(1)} %bitcast.28, bf16[2,256,256]{2,1,0:T(8,128)(2,1)S(1)} %bitcast.32), custom_call_target="tpu_custom_call" | custom-call | flops 805306368 | bytes 1835008 | tf_op jit(solution)/shard_map/pallas_call | solution.py:84
  4.6 1.9 %collective-permute-start = (bf16[6,256,256]{2,1,0:T(8,128)(2,1)S(1)}, bf16[6,256,256]{2,1,0:T(8,128)(2,1)S(1)}, u32[]{:S(2)}, u32[]{:S(2)}) collective-permute-start(bf16[6,256,256]{2,1,0:T(8,128)(2,1)S(1)} %shard_map.55), channel_id=1, source_target_pairs={{0,4},{4,0},{8,12},{12,8},{16,20},{20,16},{24,28},{28,24},{32,36},... | collective-permute-start | bytes 2359304 | tf_op jit(solution)/shard_map/ppermute | solution.py:299
  6.6 0.0 copy-start.4
  6.6 0.0 copy-start.1
  6.6 0.1 pad_maximum_fusion
  6.7 2.1 %collective-permute-done.env.once = bf16[6,256,256]{2,1,0:T(8,128)(2,1)S(1)} collective-permute-done((bf16[6,256,256]{2,1,0:T(8,128)(2,1)S(1)}, bf16[6,256,256]{2,1,0:T(8,128)(2,1)S(1)}, u32[]{:S(2)}, u32[]{:S(2)}) %collective-permute-start) | collective-permute-done | bytes 786464 | tf_op jit(solution)/shard_map/ppermute | solution.py:299
  8.8 0.6 shard_map.56
  9.3 3.2 %collective-permute-start.3 = (bf16[8,256,256]{2,1,0:T(8,128)(2,1)S(1)}, bf16[8,256,256]{2,1,0:T(8,128)(2,1)S(1)}, u32[]{:S(2)}, u32[]{:S(2)}) collective-permute-start(bf16[8,256,256]{2,1,0:T(8,128)(2,1)S(1)} %pad_maximum_fusion), channel_id=1, source_target_pairs={{0,4},{8,12},{16,20},{24,28},{32,36},{40,44},{48,52},{56,60},{64,6... | collective-permute-start | bytes 3145736 | tf_op jit(solution)/shard_map/ppermute | solution.py:306
  12.6 0.7 collective-permute-start.1
  13.3 1.3 %collective-permute-start.2 = (bf16[2,256,256]{2,1,0:T(8,128)(2,1)S(1)}, bf16[2,256,256]{2,1,0:T(8,128)(2,1)S(1)}, u32[]{:S(2)}, u32[]{:S(2)}) collective-permute-start(bf16[2,256,256]{2,1,0:T(8,128)(2,1)S(1)} %bitcast.41), channel_id=1, source_target_pairs={{4,8},{12,16},{20,24},{28,32},{36,40},{44,48},{52,56},{60,64},{68,... | collective-permute-start | bytes 786440 | tf_op jit(solution)/shard_map/ppermute | solution.py:300
  14.6 1.3 %collective-permute-start.4 = (bf16[6,160,256]{2,1,0:T(8,128)(2,1)S(1)}, bf16[6,160,256]{2,1,0:T(8,128)(2,1)S(1)}, u32[]{:S(2)}, u32[]{:S(2)}) collective-permute-start(bf16[6,160,256]{2,1,0:T(8,128)(2,1)S(1)} %slice.7), channel_id=1, source_target_pairs={{4,8},{5,9},{6,10},{7,11},{12,16},{13,17},{14,18},{15,19},{20,24},... | collective-permute-start | bytes 1474568 | tf_op jit(solution)/shard_map/ppermute | solution.py:305
  15.9 17.2 %collective-permute-done.2.last = bf16[2,256,256]{2,1,0:T(8,128)(2,1)S(1)} collective-permute-done((bf16[2,256,256]{2,1,0:T(8,128)(2,1)S(1)}, bf16[2,256,256]{2,1,0:T(8,128)(2,1)S(1)}, u32[]{:S(2)}, u32[]{:S(2)}) %collective-permute-start.2) | collective-permute-done | bytes 262176 | tf_op jit(solution)/shard_map/ppermute | solution.py:300
  33.1 0.0 collective-permute-done.1.rest_1_
  33.1 1.3 %collective-permute-start.5 = (bf16[6,96,256]{2,1,0:T(8,128)(2,1)S(1)}, bf16[6,96,256]{2,1,0:T(8,128)(2,1)S(1)}, u32[]{:S(2)}, u32[]{:S(2)}) collective-permute-start(bf16[6,96,256]{2,1,0:T(8,128)(2,1)S(1)} %collective-permute-done.1.rest_1_), channel_id=1, source_target_pairs={{508,256},{509,257},{510,258},{511,259},{252,0},{253,1},{254,2},{2... | collective-permute-start | bytes 884744 | tf_op jit(solution)/shard_map/ppermute | solution.py:308
  34.4 0.0 collective-permute-done.3.partner_env
  34.4 2.7 %shard_map.57 = (bf16[4,1536,256]{2,1,0:T(8,128)(2,1)S(1)}, f32[4,64,256]{2,1,0:T(8,128)S(1)}, bf16[4,4,64,256]{3,2,1,0:T(8,128)(2,1)S(1)}, bf16[6,256,256]{2,1,0:T(8,128)(2,1)S(1)}) custom-call(s32[3]{0:T(128)S(1)} %pad_add_fusion.place, s32[2,6]{1,0:T(2,128)S(1)} %bitcast.38, bf16[2,256,256]{2,1,0:T(8,128)(2,1)S(1)} %collective-permute-done.2.last, ...), custom_call_target="tpu_custom_call" | custom-call | flops 939524096 | bytes 6553600 | tf_op jit(solution)/shard_map/pallas_call | solution.py:148
  37.2 6.1 %collective-permute-done.4.rest_0_ = bf16[6,160,256]{2,1,0:T(8,128)(2,1)S(1)} collective-permute-done((bf16[6,160,256]{2,1,0:T(8,128)(2,1)S(1)}, bf16[6,160,256]{2,1,0:T(8,128)(2,1)S(1)}, u32[]{:S(2)}, u32[]{:S(2)}) %collective-permute-start.4) | collective-permute-done | bytes 491552 | tf_op jit(solution)/shard_map/ppermute | solution.py:305
  43.3 2.5 %collective-permute-done.5.rest_2_ = bf16[6,96,256]{2,1,0:T(8,128)(2,1)S(1)} collective-permute-done((bf16[6,96,256]{2,1,0:T(8,128)(2,1)S(1)}, bf16[6,96,256]{2,1,0:T(8,128)(2,1)S(1)}, u32[]{:S(2)}, u32[]{:S(2)}) %collective-permute-start.5) | collective-permute-done | bytes 294944 | tf_op jit(solution)/shard_map/ppermute | solution.py:308
  45.8 1.5 %shard_map.58 = (bf16[4,4,64,256]{3,2,1,0:T(8,128)(2,1)S(1)}, bf16[6,256,256]{2,1,0:T(8,128)(2,1)S(1)}) custom-call(s32[3]{0:T(128)S(1)} %pad_add_fusion.place, bf16[4,1536,256]{2,1,0:T(8,128)(2,1)S(1)} %get-tuple-element.21.applied, bf16[4,4,64,256]{3,2,1,0:T(8,128)(2,1)S(1)} %get-tuple-element.22.before, ...), custom_call_target="tpu_custom_call" | custom-call | flops 805306368 | bytes 4718592 | tf_op jit(solution)/shard_map/pallas_call | solution.py:195
  47.3 16.2 %all_to_all.10 = bf16[4,4,64,256]{3,2,1,0:T(8,128)(2,1)S(1)} all-to-all(bf16[4,4,64,256]{3,2,1,0:T(8,128)(2,1)S(1)} %get-tuple-element.24), channel_id=1, replica_groups=mesh['sec'=128,'term'=4] {'term'}, dimensions={0} | all-to-all | bytes 1048576 | tf_op jit(solution)/shard_map/all_to_all | solution.py:316
  63.5 0.1 convert_reduce_fusion.1
  63.6 16.1 %all-gather = bf16[16,64,256]{2,1,0:T(8,128)(2,1)S(1)} all-gather(bf16[4,64,256]{2,1,0:T(8,128)(2,1)S(1)} %fusion), channel_id=2, replica_groups=mesh['sec'=128,'term'=4] {'term'}, dimensions={0}, use_global_device_ids=true | all-gather | bytes 655360 | tf_op jit(solution)/shard_map/all_gather | solution.py:318
  79.7 2.6 %shard_map.59 = bf16[4,4,64,256]{3,2,1,0:T(8,128)(2,1)S(1)} custom-call(s32[3]{0:T(128)S(1)} %pad_add_fusion.place, s32[2,6]{1,0:T(2,128)S(1)} %bitcast.39, bf16[4,4,64,256]{3,2,1,0:T(8,128)(2,1)S(1)} %bitcast.31, bf16[6,256,256]{2,1,0:T(8,128)(2,1)S(1)} %get-tuple-element.25.left_env, bf16[6,256,256]{2,1,0:T(8,128)(2,1)S(1)} %get-tuple-element.26.right_env), custom_call_target="tpu_custom_call" | custom-call | flops 1610612736 | bytes 3145728 | tf_op jit(solution)/shard_map/pallas_call | solution.py:220
  82.4 12.7 %all_to_all.11 = bf16[4,4,64,256]{3,2,1,0:T(8,128)(2,1)S(1)} all-to-all(bf16[4,4,64,256]{3,2,1,0:T(8,128)(2,1)S(1)} %shard_map.59), channel_id=1, replica_groups=mesh['sec'=128,'term'=4] {'term'}, dimensions={0} | all-to-all | bytes 1048576 | tf_op jit(solution)/shard_map/all_to_all | solution.py:320
  95.0 0.1 convert_reduce_fusion
  95.1 0.1 subtract_convert_fusion
  95.2 14.7 %all-gather.1 = bf16[16,64,256]{2,1,0:T(8,128)(2,1)S(1)} all-gather(bf16[4,64,256]{2,1,0:T(8,128)(2,1)S(1)} %subtract_convert_fusion), channel_id=3, replica_groups=mesh['sec'=128,'term'=4] {'term'}, dimensions={0}, use_global_device_ids=true | all-gather | bytes 655360 | tf_op jit(solution)/shard_map/all_gather | solution.py:322
  109.8 1.3 %shard_map.60 = f32[2048,128]{1,0:T(8,128)} custom-call(bf16[4,4,64,256]{3,2,1,0:T(8,128)(2,1)S(1)} %bitcast.27), custom_call_target="tpu_custom_call" | custom-call | bytes 1572864 | tf_op jit(solution)/shard_map/pallas_call | solution.py:258
  (11 shorter events, 0.2 us)
Async XLA Ops:
  0.0 6.5 %copy-start.3 = (bf16[1,256,2,256]{3,2,1,0:T(2,128)(2,1)S(1)}, bf16[1,256,2,256]{3,2,1,0:T(2,128)(2,1)}, u32[]{:S(2)}) copy-start(bf16[1,256,2,256]{3,2,1,0:T(2,128)(2,1)} %param.7) | copy-start | bytes 786436
  1.1 1.1 %copy-start = (bf16[1,6,256,256]{3,2,1,0:T(8,128)(2,1)S(1)}, bf16[1,6,256,256]{3,2,1,0:T(8,128)(2,1)}, u32[]{:S(2)}) copy-start(bf16[1,6,256,256]{3,2,1,0:T(8,128)(2,1)} %param.5) | copy-start | bytes 2359300
  2.2 0.7 copy-start.2
  4.6 4.2 %collective-permute-start = (bf16[6,256,256]{2,1,0:T(8,128)(2,1)S(1)}, bf16[6,256,256]{2,1,0:T(8,128)(2,1)S(1)}, u32[]{:S(2)}, u32[]{:S(2)}) collective-permute-start(bf16[6,256,256]{2,1,0:T(8,128)(2,1)S(1)} %shard_map.55), channel_id=1, source_target_pairs={{0,4},{4,0},{8,12},{12,8},{16,20},{20,16},{24,28},{28,24},{32,36},... | collective-permute-start | bytes 2359304 | tf_op jit(solution)/shard_map/ppermute | solution.py:299
  6.6 27.8 %copy-start.4 = (bf16[1,256,2,256]{3,2,1,0:T(2,128)(2,1)S(1)}, bf16[1,256,2,256]{3,2,1,0:T(2,128)(2,1)}, u32[]{:S(2)}) copy-start(bf16[1,256,2,256]{3,2,1,0:T(2,128)(2,1)} %param.8) | copy-start | bytes 786436
  6.6 27.9 %copy-start.1 = (bf16[1,6,256,256]{3,2,1,0:T(8,128)(2,1)S(1)}, bf16[1,6,256,256]{3,2,1,0:T(8,128)(2,1)}, u32[]{:S(2)}) copy-start(bf16[1,6,256,256]{3,2,1,0:T(8,128)(2,1)} %param.5) | copy-start | bytes 2359300
  9.3 25.1 %collective-permute-start.3 = (bf16[8,256,256]{2,1,0:T(8,128)(2,1)S(1)}, bf16[8,256,256]{2,1,0:T(8,128)(2,1)S(1)}, u32[]{:S(2)}, u32[]{:S(2)}) collective-permute-start(bf16[8,256,256]{2,1,0:T(8,128)(2,1)S(1)} %pad_maximum_fusion), channel_id=1, source_target_pairs={{0,4},{8,12},{16,20},{24,28},{32,36},{40,44},{48,52},{56,60},{64,6... | collective-permute-start | bytes 3145736 | tf_op jit(solution)/shard_map/ppermute | solution.py:306
  12.6 20.5 %collective-permute-start.1 = (bf16[6,96,256]{2,1,0:T(8,128)(2,1)S(1)}, bf16[6,96,256]{2,1,0:T(8,128)(2,1)S(1)}, u32[]{:S(2)}, u32[]{:S(2)}) collective-permute-start(bf16[6,96,256]{2,1,0:T(8,128)(2,1)S(1)} %slice.6), channel_id=1, source_target_pairs={{4,8},{5,9},{6,10},{7,11},{12,16},{13,17},{14,18},{15,19},{20,24},... | collective-permute-start | bytes 884744 | tf_op jit(solution)/shard_map/ppermute | solution.py:304
  13.3 19.8 %collective-permute-start.2 = (bf16[2,256,256]{2,1,0:T(8,128)(2,1)S(1)}, bf16[2,256,256]{2,1,0:T(8,128)(2,1)S(1)}, u32[]{:S(2)}, u32[]{:S(2)}) collective-permute-start(bf16[2,256,256]{2,1,0:T(8,128)(2,1)S(1)} %bitcast.41), channel_id=1, source_target_pairs={{4,8},{12,16},{20,24},{28,32},{36,40},{44,48},{52,56},{60,64},{68,... | collective-permute-start | bytes 786440 | tf_op jit(solution)/shard_map/ppermute | solution.py:300
  14.6 28.7 %collective-permute-start.4 = (bf16[6,160,256]{2,1,0:T(8,128)(2,1)S(1)}, bf16[6,160,256]{2,1,0:T(8,128)(2,1)S(1)}, u32[]{:S(2)}, u32[]{:S(2)}) collective-permute-start(bf16[6,160,256]{2,1,0:T(8,128)(2,1)S(1)} %slice.7), channel_id=1, source_target_pairs={{4,8},{5,9},{6,10},{7,11},{12,16},{13,17},{14,18},{15,19},{20,24},... | collective-permute-start | bytes 1474568 | tf_op jit(solution)/shard_map/ppermute | solution.py:305
  33.1 12.7 %collective-permute-start.5 = (bf16[6,96,256]{2,1,0:T(8,128)(2,1)S(1)}, bf16[6,96,256]{2,1,0:T(8,128)(2,1)S(1)}, u32[]{:S(2)}, u32[]{:S(2)}) collective-permute-start(bf16[6,96,256]{2,1,0:T(8,128)(2,1)S(1)} %collective-permute-done.1.rest_1_), channel_id=1, source_target_pairs={{508,256},{509,257},{510,258},{511,259},{252,0},{253,1},{254,2},{2... | collective-permute-start | bytes 884744 | tf_op jit(solution)/shard_map/ppermute | solution.py:308

commit v3 on v2

v3 whole, which is shorter than its diff:
```python
import functools

import jax
import jax.numpy as jnp
from jax import lax
from jax.experimental import pallas as pl
from jax.experimental.pallas import tpu as pltpu
from jax.sharding import PartitionSpec as P

STEP = 0.2
EPS = 1e-06
F32 = jnp.float32
BF16 = jnp.bfloat16

FIXED = 3
ROW = 16
CUT = 10

VMEM = pl.BlockSpec(memory_space=pltpu.VMEM)
SMEM = pl.BlockSpec(memory_space=pltpu.SMEM)


def nn(a, b):
    return lax.dot_general(a, b, (((1,), (0,)), ((), ())), preferred_element_type=F32)


def nt(a, b):
    return lax.dot_general(a, b, (((1,), (1,)), ((), ())), preferred_element_type=F32)


def identity(n):
    rows = lax.broadcasted_iota(jnp.int32, (n, n), 0)
    cols = lax.broadcasted_iota(jnp.int32, (n, n), 1)
    return (rows == cols).astype(F32).astype(BF16)


def call(body, out_shape, specs, scratch=(), flops=0, nbytes=0, aliases=None, mib=20):
    outs = out_shape if isinstance(out_shape, (tuple, list)) else (out_shape,)
    out_specs = [VMEM] * len(outs)
    return pl.pallas_call(
        body,
        out_shape=list(outs),
        in_specs=list(specs),
        out_specs=out_specs,
        scratch_shapes=list(scratch),
        input_output_aliases=aliases or {},
        compiler_params=pltpu.CompilerParams(vmem_limit_bytes=mib * 2**20),
        cost_estimate=pl.CostEstimate(flops=flops, bytes_accessed=nbytes, transcendentals=0),
    )


def extend(plain, facts, env, iso, wide, out):
    terms, bond, _ = env.shape
    levels = [iso[s] for s in range(2)]
    if plain:
        eye = identity(bond)
        back = jnp.concatenate([nt(eye, level).astype(BF16) for level in levels], axis=1)
    else:
        back = jnp.concatenate(levels, axis=1)
    for k in range(terms):
        kind = facts[FIXED + (0 if plain else terms) + k]
        crossed = lax.rem(kind, 2) == 1
        lower = jnp.where(kind >= 2, -1.0, 1.0).astype(F32)
        value = env[k]
        left, right = [nn(value, level) if plain else nt(value, level) for level in levels]
        wide[k, :bond] = jnp.where(crossed, right, left).astype(BF16)
        wide[k, bond:] = (jnp.where(crossed, left, right) * lower).astype(BF16)
    for k in range(terms):
        out[k] = nn(back, wide[k]).astype(BF16)


def extend_first_body(facts, env, iso, out, wide):
    for odd in range(2):

        @pl.when(facts[0] == odd)
        def _():
            extend(odd == 0, facts, env, iso, wide, out)


def extend_odd_body(facts, env, iso, out, wide):
    @pl.when(facts[0] == 1)
    def _():
        extend(True, facts, env, iso, wide, out)


def extend_call(body, facts, env, iso):
    terms, bond, _ = env.shape
    return call(
        body,
        jax.ShapeDtypeStruct(env.shape, BF16),
        [SMEM, VMEM, VMEM],
        [pltpu.VMEM((terms, 2 * bond, bond), BF16)],
        flops=terms * 8 * bond**3,
        nbytes=4 * terms * bond * bond + 4 * bond * bond,
    )(facts, env, iso)[0]


def store_right(facts, terms, k, vector, right, applied):
    bond = right.shape[0]
    kind0, kind1 = facts[FIXED + k], facts[FIXED + terms + k]
    mask = 2 * lax.rem(kind0, 2) + lax.rem(kind1, 2)
    lower0 = jnp.where(kind0 >= 2, -1.0, 1.0).astype(F32)
    lower1 = jnp.where(kind1 >= 2, -1.0, 1.0).astype(F32)
    for y in range(4):
        part = nt(vector[y], right)
        x = y ^ mask
        sign = jnp.where(x >= 2, lower0, 1.0) * jnp.where(lax.rem(x, 2) == 1, lower1, 1.0)
        applied[x, k * bond : (k + 1) * bond, :] = (part * sign).astype(BF16)


def store_left(lefts, applied, out):
    size, _, rows, _ = out.shape
    joined = jnp.concatenate(lefts, axis=1)
    for x in range(4):
        part = nn(joined, applied[x]).astype(BF16)
        for q in range(size):
            out[q, x] = part[q * rows : (q + 1) * rows]


def first_body(facts, last, first, own_env, partner, once, iso, *rest):
    applied, share, out, right_env, exact, vector, wide = rest
    terms, bond, _ = own_env.shape
    rows = share.shape[1]
    for s in range(2):
        for t in range(2):
            value = nn(last[s], first[t])
            exact[2 * s + t] = value
            vector[2 * s + t] = value.astype(BF16)
    start = pl.multiple_of(facts[1] * rows, rows)
    for x in range(4):
        share[x] = exact[x, pl.ds(start, rows), :]

    @pl.when(facts[0] == 1)
    def _():
        for k in range(terms):
            right = own_env[k]
            right_env[k] = right
            store_right(facts, terms, k, vector, right, applied)
        store_left([partner[k] for k in range(terms)], applied, out)

    @pl.when(facts[0] == 0)
    def _():
        extend(False, facts, once, iso, wide, right_env)
        for k in range(terms):
            store_right(facts, terms, k, vector, right_env[k], applied)


def first_call(size, facts, last, first, own_env, partner, once, iso):
    terms, bond, _ = own_env.shape
    rows = bond // size
    return call(
        first_body,
        [
            jax.ShapeDtypeStruct((4, terms * bond, bond), BF16),
            jax.ShapeDtypeStruct((4, rows, bond), F32),
            jax.ShapeDtypeStruct((size, 4, rows, bond), BF16),
            jax.ShapeDtypeStruct(own_env.shape, BF16),
        ],
        [SMEM] + [VMEM] * 6,
        [
            pltpu.VMEM((4, bond, bond), F32),
            pltpu.VMEM((4, bond, bond), BF16),
            pltpu.VMEM((terms, 2 * bond, bond), BF16),
        ],
        flops=4000 * bond**3,
    )(facts, last, first, own_env, partner, once, iso)


def second_body(facts, applied, before, partner, came, piece, relayed, out, left_env):
    terms = left_env.shape[0]
    cut = came.shape[1]

    @pl.when(facts[0] == 0)
    def _():
        for k in range(terms):
            left_env[k, :cut] = came[k]
            left_env[k, cut:] = jnp.where(facts[2] == 1, relayed[k], piece[k])
        store_left([left_env[k] for k in range(terms)], applied, out)

    @pl.when(facts[0] == 1)
    def _():
        for k in range(terms):
            left_env[k] = partner[k]
        for q in range(out.shape[0]):
            out[q] = before[q]


def second_call(facts, applied, before, partner, came, piece, relayed):
    terms, _, bond = came.shape
    return call(
        second_body,
        [
            jax.ShapeDtypeStruct(before.shape, BF16),
            jax.ShapeDtypeStruct((terms, bond, bond), BF16),
        ],
        [SMEM] + [VMEM] * 6,
        flops=8 * terms * bond**3,
        nbytes=14 * terms * bond * bond,
    )(facts, applied, before, partner, came, piece, relayed)


def apply_body(facts, gathered, left_env, right_env, out, vector, applied):
    size, _, rows, bond = gathered.shape
    terms = left_env.shape[0]
    for q in range(size):
        for x in range(4):
            vector[x, q * rows : (q + 1) * rows, :] = gathered[q, x]
    for k in range(terms):
        store_right(facts, terms, k, vector, right_env[k], applied)
    store_left([left_env[k] for k in range(terms)], applied, out)


def apply_call(facts, gathered, left_env, right_env):
    terms, bond, _ = left_env.shape
    return call(
        apply_body,
        jax.ShapeDtypeStruct(gathered.shape, BF16),
        [SMEM] + [VMEM] * 3,
        [pltpu.VMEM((4, bond, bond), BF16), pltpu.VMEM((4, terms * bond, bond), BF16)],
        flops=16 * terms * bond**3,
        nbytes=8 * terms * bond * bond,
    )(facts, gathered, left_env, right_env)[0]


def update(parts, share):
    share = share - STEP * jnp.sum(parts.astype(F32), axis=0)
    return share, share.astype(BF16)


def final_body(gathered, out):
    size, _, rows, bond = gathered.shape
    total = jnp.zeros((rows, bond), F32)
    for q in range(size):
        for x in range(4):
            value = gathered[q, x].astype(F32)
            total = total + value * value
    mean = jnp.sum(total) / (size * 4 * rows * bond)
    scale = lax.rsqrt(jnp.full((8, 128), mean + EPS, F32))[0:1, 0:1]
    halves = bond // 128
    pitch = 4 * halves
    for q in range(size):
        for x in range(4):
            value = gathered[q, x].astype(F32) * scale
            s, t = x // 2, x % 2
            for j in range(halves):
                begin = q * rows * pitch + s * 2 * halves + j * 2 + t
                out[pl.ds(begin, rows, stride=pitch), :] = value[:, j * 128 : (j + 1) * 128]


def final_call(gathered):
    size, _, rows, bond = gathered.shape
    halves = bond // 128
    flat = call(
        final_body,
        jax.ShapeDtypeStruct((size * rows * 4 * halves, 128), F32),
        [VMEM],
        nbytes=gathered.size * 6,
    )(gathered)[0]
    blocks = flat.reshape(size * rows, 2, halves, 2, 128)
    return jnp.transpose(blocks, (0, 1, 3, 2, 4)).reshape(1, size * rows, 2, 2, bond)


def levels_first(site):
    return jnp.transpose(site, (1, 0, 2))


def shards(meet_env, meet_iso, last_site, first_site, term_kind):
    sections, size = lax.axis_size("sec"), lax.axis_size("term")
    own_env = meet_env[0]
    section = lax.axis_index("sec")
    odd = section % 2
    far = (section % (sections // 2) == 0).astype(jnp.int32)
    facts = jnp.stack([odd, lax.axis_index("term"), far])
    facts = jnp.concatenate([facts.astype(jnp.int32), term_kind[:, 0], term_kind[:, 1]])
    bond = own_env.shape[1]

    swap = [(i, i ^ 1) for i in range(sections)]
    to_odd = [(i, i + 1) for i in range(0, sections, 2)]
    onward = [(i, (i + 1) % sections) for i in range(sections)]
    odd_on = [(i, (i + 1) % sections) for i in range(1, sections, 2)]

    half = sections // 2
    row = min(ROW, half)
    ends = [half - 1, sections - 1]
    by_row = [(i, j) for i, j in odd_on if i not in ends] + [(i, i - half + row) for i in ends]
    then_on = [(i - half + row, (i + 1) % sections) for i in ends]

    own_iso = levels_first(meet_iso[0])
    own_last = levels_first(last_site[0])
    once = extend_call(extend_first_body, facts, own_env, own_iso)
    raw_env, once = lax.optimization_barrier((own_env, once))
    once = lax.ppermute(once, "sec", swap)
    partner = lax.ppermute(raw_env, "sec", to_odd)
    last = lax.ppermute(own_last, "sec", onward)
    fresh = extend_call(extend_odd_body, facts, once, own_iso)
    cut = CUT * bond // 16
    came = lax.ppermute(fresh[:, :cut], "sec", odd_on)
    piece = lax.ppermute(fresh[:, cut:], "sec", by_row)
    relayed = lax.ppermute(piece, "sec", then_on)
    first = levels_first(first_site[0])
    applied, share, summand, right_env = first_call(
        size, facts, last, first, own_env, partner, once, own_iso
    )
    summand, left_env = second_call(
        facts, applied, summand, partner, came, piece, relayed
    )
    parts = lax.all_to_all(summand, "term", 0, 0, tiled=True)
    share, rounded = update(parts, share)
    gathered = lax.all_gather(rounded, "term")
    summand = apply_call(facts, gathered, left_env, right_env)
    parts = lax.all_to_all(summand, "term", 0, 0, tiled=True)
    share, rounded = update(parts, share)
    gathered = lax.all_gather(rounded, "term")
    return final_call(gathered)


def solution(mesh):
    in_specs = (
        P("sec", "term", None, None),
        P("sec", None, None, None),
        P("sec", None, None, None),
        P("sec", None, None, None),
        P("term", None),
    )
    out_specs = P("sec", None, None, None, None)
    return jax.shard_map(shards, mesh=mesh, in_specs=in_specs, out_specs=out_specs, check_vma=False)
```

time: 112 us -> 109 us (0.973)
  the two profiles are of different devices: /device:TPU:256 before, /device:TPU:64 now
where the time goes in v3:
time: 109 us
  blocking collectives  59.7 us (55%)
  waiting for transfers between devices  22.7 us (21%)
  starting transfers between devices  12.5 us (11%)
  Pallas kernels  11.6 us (11%)
  local copies, waits for them, and re-layouts  1.93 us (2%)
    all_gather x2, blocking collectives, shards(): gathered = lax.all_gather(rounded, 'term')  29.9 us
    all_to_all x2, blocking collectives, shards(): parts = lax.all_to_all(summand, 'term', 0, 0, tiled=True)  29.8 us
    ppermute x1, waiting for transfers between devices, shards(): last = lax.ppermute(own_last, 'sec', onward)  15.6 us
    ppermute x1, waiting for transfers between devices, shards(): came = lax.ppermute(fresh[:, :cut], 'sec', odd_on)  7.09 us
    ppermute x1, starting transfers between devices, shards(): last = lax.ppermute(own_last, 'sec', onward)  4.84 us
    pallas_call x1, Pallas kernels, first_call(): call(first_body, [jax.ShapeDtypeStruct((4, terms * bond, bond), BF16), ja...  3.33 us
    pallas_call x2, Pallas kernels, extend_call(): call(body, jax.ShapeDtypeStruct(env.shape, BF16), [SMEM, VMEM, VMEM], [pl...  2.86 us
    pallas_call x1, Pallas kernels, apply_call(): call(apply_body, jax.ShapeDtypeStruct(gathered.shape, BF16), [SMEM] + [VM...  2.58 us
  transfers between devices with their start and end apart: 6, of which 2 were waited for; matrix products, arithmetic and copies ran while one was open for 0% of the time, Pallas kernels for 4%

profile of v3, /device:TPU:64, one launch (start us, length us, event | category | flops | bytes accessed | tf_op | source)
XLA Modules:
  0.0 108.9 jit_solution(17307881640716360203)
XLA Ops:
  0.0 0.8 slice_bitcast_fusion
  0.8 1.0 copy.17
  1.7 0.1 concatenate.3.facts
  1.8 0.0 copy-start
  1.8 0.0 copy-start.1
  1.8 2.3 %shard_map.55 = bf16[6,256,256]{2,1,0:T(8,128)(2,1)S(1)} custom-call(s32[15]{0:T(128)S(1)} %concatenate.3.facts, bf16[6,256,256]{2,1,0:T(8,128)(2,1)} %bitcast.9.env.own_env, bf16[2,256,256]{2,1,0:T(8,128)(2,1)S(1)} %bitcast.32), custom_call_target="tpu_custom_call" | custom-call | flops 805306368 | bytes 1835008 | tf_op jit(solution)/shard_map/pallas_call | solution.py:88
  4.1 1.9 %collective-permute-start.2 = (bf16[6,256,256]{2,1,0:T(8,128)(2,1)S(1)}, bf16[6,256,256]{2,1,0:T(8,128)(2,1)S(1)}, u32[]{:S(2)}, u32[]{:S(2)}) collective-permute-start(bf16[6,256,256]{2,1,0:T(8,128)(2,1)S(1)} %shard_map.55), channel_id=1, source_target_pairs={{0,4},{4,0},{8,12},{12,8},{16,20},{20,16},{24,28},{28,24},{32,36},... | collective-permute-start | bytes 2359304 | tf_op jit(solution)/shard_map/ppermute | solution.py:292
  6.1 2.5 %collective-permute-start.1 = (bf16[6,256,256]{2,1,0:T(8,128)(2,1)}, bf16[6,256,256]{2,1,0:T(8,128)(2,1)S(1)}, u32[]{:S(2)}, u32[]{:S(2)}) collective-permute-start(bf16[6,256,256]{2,1,0:T(8,128)(2,1)} %bitcast.9.env.own_env), channel_id=1, source_target_pairs={{0,4},{8,12},{16,20},{24,28},{32,36},{40,44},{48,52},{56,60},{64,6... | collective-permute-start | bytes 2359304 | tf_op jit(solution)/shard_map/ppermute | solution.py:293
  8.5 0.0 collective-permute-done.2.once.env
  8.5 0.5 shard_map.57
  9.1 0.7 collective-permute-start.4
  9.8 0.0 copy-done
  9.9 4.8 %collective-permute-start = (bf16[2,256,256]{2,1,0:T(8,128)(2,1)S(1)}, bf16[2,256,256]{2,1,0:T(8,128)(2,1)S(1)}, u32[]{:S(2)}, u32[]{:S(2)}) collective-permute-start(bf16[2,256,256]{2,1,0:T(8,128)(2,1)S(1)} %bitcast.36), channel_id=1, source_target_pairs={{0,4},{4,8},{8,12},{12,16},{16,20},{20,24},{24,28},{28,32},{32,36}... | collective-permute-start | bytes 786440 | tf_op jit(solution)/shard_map/ppermute | solution.py:294
  14.7 0.0 copy-done.1
  14.8 1.3 %collective-permute-start.3 = (bf16[6,160,256]{2,1,0:T(8,128)(2,1)S(1)}, bf16[6,160,256]{2,1,0:T(8,128)(2,1)S(1)}, u32[]{:S(2)}, u32[]{:S(2)}) collective-permute-start(bf16[6,160,256]{2,1,0:T(8,128)(2,1)S(1)} %slice.16), channel_id=1, source_target_pairs={{4,8},{12,16},{20,24},{28,32},{36,40},{44,48},{52,56},{60,64},{68,... | collective-permute-start | bytes 1474568 | tf_op jit(solution)/shard_map/ppermute | solution.py:297
  16.1 0.0 collective-permute-done.4.piece
  16.1 1.3 %collective-permute-start.5 = (bf16[6,96,256]{2,1,0:T(8,128)(2,1)S(1)}, bf16[6,96,256]{2,1,0:T(8,128)(2,1)S(1)}, u32[]{:S(2)}, u32[]{:S(2)}) collective-permute-start(bf16[6,96,256]{2,1,0:T(8,128)(2,1)S(1)} %collective-permute-done.4.piece), channel_id=1, source_target_pairs={{60,256},{316,0},{61,257},{317,1},{62,258},{318,2},{63,259},{319,3}} | collective-permute-start | bytes 884744 | tf_op jit(solution)/shard_map/ppermute | solution.py:299
  17.4 15.6 %collective-permute-done.last = bf16[2,256,256]{2,1,0:T(8,128)(2,1)S(1)} collective-permute-done((bf16[2,256,256]{2,1,0:T(8,128)(2,1)S(1)}, bf16[2,256,256]{2,1,0:T(8,128)(2,1)S(1)}, u32[]{:S(2)}, u32[]{:S(2)}) %collective-permute-start) | collective-permute-done | bytes 262176 | tf_op jit(solution)/shard_map/ppermute | solution.py:294
  33.1 0.0 collective-permute-done.1.partner
  33.1 3.3 %shard_map.56 = (bf16[4,1536,256]{2,1,0:T(8,128)(2,1)S(1)}, f32[4,64,256]{2,1,0:T(8,128)S(1)}, bf16[4,4,64,256]{3,2,1,0:T(8,128)(2,1)S(1)}, bf16[6,256,256]{2,1,0:T(8,128)(2,1)S(1)}) custom-call(s32[15]{0:T(128)S(1)} %concatenate.3.facts, bf16[2,256,256]{2,1,0:T(8,128)(2,1)S(1)} %collective-permute-done.last, bf16[2,256,256]{2,1,0:T(8,128)(2,1)S(1)} %bitcast.35, ...), custom_call_target="tpu_custom_call" | custom-call | flops 67108864000 | tf_op jit(solution)/shard_map/pallas_call | solution.py:151
  36.4 7.1 %collective-permute-done.3.came = bf16[6,160,256]{2,1,0:T(8,128)(2,1)S(1)} collective-permute-done((bf16[6,160,256]{2,1,0:T(8,128)(2,1)S(1)}, bf16[6,160,256]{2,1,0:T(8,128)(2,1)S(1)}, u32[]{:S(2)}, u32[]{:S(2)}) %collective-permute-start.3) | collective-permute-done | bytes 491552 | tf_op jit(solution)/shard_map/ppermute | solution.py:297
  43.5 0.0 collective-permute-done.5.relayed
  43.5 1.5 %shard_map.58 = (bf16[4,4,64,256]{3,2,1,0:T(8,128)(2,1)S(1)}, bf16[6,256,256]{2,1,0:T(8,128)(2,1)S(1)}) custom-call(s32[15]{0:T(128)S(1)} %concatenate.3.facts, bf16[4,1536,256]{2,1,0:T(8,128)(2,1)S(1)} %get-tuple-element.16.applied, bf16[4,4,64,256]{3,2,1,0:T(8,128)(2,1)S(1)} %get-tuple-element.17.before, ...), custom_call_target="tpu_custom_call" | custom-call | flops 805306368 | bytes 5505024 | tf_op jit(solution)/shard_map/pallas_call | solution.py:190
  45.0 16.2 %all_to_all.10 = bf16[4,4,64,256]{3,2,1,0:T(8,128)(2,1)S(1)} all-to-all(bf16[4,4,64,256]{3,2,1,0:T(8,128)(2,1)S(1)} %get-tuple-element.18), channel_id=1, replica_groups=mesh['sec'=128,'term'=4] {'term'}, dimensions={0} | all-to-all | bytes 1048576 | tf_op jit(solution)/shard_map/all_to_all | solution.py:307
  61.3 0.1 convert_reduce_fusion.1
  61.4 15.5 %all-gather = bf16[16,64,256]{2,1,0:T(8,128)(2,1)S(1)} all-gather(bf16[4,64,256]{2,1,0:T(8,128)(2,1)S(1)} %fusion), channel_id=2, replica_groups=mesh['sec'=128,'term'=4] {'term'}, dimensions={0}, use_global_device_ids=true | all-gather | bytes 655360 | tf_op jit(solution)/shard_map/all_gather | solution.py:309
  76.9 2.6 %shard_map.59 = bf16[4,4,64,256]{3,2,1,0:T(8,128)(2,1)S(1)} custom-call(s32[15]{0:T(128)S(1)} %concatenate.3.facts, bf16[4,4,64,256]{3,2,1,0:T(8,128)(2,1)S(1)} %bitcast.31, bf16[6,256,256]{2,1,0:T(8,128)(2,1)S(1)} %get-tuple-element.19.left_env, bf16[6,256,256]{2,1,0:T(8,128)(2,1)S(1)} %get-tuple-element.20.right_env), custom_call_target="tpu_custom_call" | custom-call | flops 1610612736 | bytes 3145728 | tf_op jit(solution)/shard_map/pallas_call | solution.py:215
  79.5 13.5 %all_to_all.11 = bf16[4,4,64,256]{3,2,1,0:T(8,128)(2,1)S(1)} all-to-all(bf16[4,4,64,256]{3,2,1,0:T(8,128)(2,1)S(1)} %shard_map.59), channel_id=1, replica_groups=mesh['sec'=128,'term'=4] {'term'}, dimensions={0} | all-to-all | bytes 1048576 | tf_op jit(solution)/shard_map/all_to_all | solution.py:311
  93.0 0.1 convert_reduce_fusion
  93.1 0.1 subtract_convert_fusion
  93.2 14.4 %all-gather.1 = bf16[16,64,256]{2,1,0:T(8,128)(2,1)S(1)} all-gather(bf16[4,64,256]{2,1,0:T(8,128)(2,1)S(1)} %subtract_convert_fusion), channel_id=3, replica_groups=mesh['sec'=128,'term'=4] {'term'}, dimensions={0}, use_global_device_ids=true | all-gather | bytes 655360 | tf_op jit(solution)/shard_map/all_gather | solution.py:313
  107.6 1.3 %shard_map.60 = f32[2048,128]{1,0:T(8,128)} custom-call(bf16[4,4,64,256]{3,2,1,0:T(8,128)(2,1)S(1)} %bitcast.30), custom_call_target="tpu_custom_call" | custom-call | bytes 1572864 | tf_op jit(solution)/shard_map/pallas_call | solution.py:253
  (5 shorter events, 0.2 us)
Async XLA Ops:
  1.8 8.0 %copy-start = (bf16[1,256,2,256]{3,2,1,0:T(2,128)(2,1)S(1)}, bf16[1,256,2,256]{3,2,1,0:T(2,128)(2,1)}, u32[]{:S(2)}) copy-start(bf16[1,256,2,256]{3,2,1,0:T(2,128)(2,1)} %param.7) | copy-start | bytes 786436
  1.8 12.9 %copy-start.1 = (bf16[1,256,2,256]{3,2,1,0:T(2,128)(2,1)S(1)}, bf16[1,256,2,256]{3,2,1,0:T(2,128)(2,1)}, u32[]{:S(2)}) copy-start(bf16[1,256,2,256]{3,2,1,0:T(2,128)(2,1)} %param.8) | copy-start | bytes 786436
  4.1 4.4 %collective-permute-start.2 = (bf16[6,256,256]{2,1,0:T(8,128)(2,1)S(1)}, bf16[6,256,256]{2,1,0:T(8,128)(2,1)S(1)}, u32[]{:S(2)}, u32[]{:S(2)}) collective-permute-start(bf16[6,256,256]{2,1,0:T(8,128)(2,1)S(1)} %shard_map.55), channel_id=1, source_target_pairs={{0,4},{4,0},{8,12},{12,8},{16,20},{20,16},{24,28},{28,24},{32,36},... | collective-permute-start | bytes 2359304 | tf_op jit(solution)/shard_map/ppermute | solution.py:292
  6.1 27.0 %collective-permute-start.1 = (bf16[6,256,256]{2,1,0:T(8,128)(2,1)}, bf16[6,256,256]{2,1,0:T(8,128)(2,1)S(1)}, u32[]{:S(2)}, u32[]{:S(2)}) collective-permute-start(bf16[6,256,256]{2,1,0:T(8,128)(2,1)} %bitcast.9.env.own_env), channel_id=1, source_target_pairs={{0,4},{8,12},{16,20},{24,28},{32,36},{40,44},{48,52},{56,60},{64,6... | collective-permute-start | bytes 2359304 | tf_op jit(solution)/shard_map/ppermute | solution.py:293
  9.1 7.0 %collective-permute-start.4 = (bf16[6,96,256]{2,1,0:T(8,128)(2,1)S(1)}, bf16[6,96,256]{2,1,0:T(8,128)(2,1)S(1)}, u32[]{:S(2)}, u32[]{:S(2)}) collective-permute-start(bf16[6,96,256]{2,1,0:T(8,128)(2,1)S(1)} %slice.17), channel_id=1, source_target_pairs={{4,8},{12,16},{20,24},{28,32},{36,40},{44,48},{52,56},{60,64},{68,... | collective-permute-start | bytes 884744 | tf_op jit(solution)/shard_map/ppermute | solution.py:298
  9.9 23.2 %collective-permute-start = (bf16[2,256,256]{2,1,0:T(8,128)(2,1)S(1)}, bf16[2,256,256]{2,1,0:T(8,128)(2,1)S(1)}, u32[]{:S(2)}, u32[]{:S(2)}) collective-permute-start(bf16[2,256,256]{2,1,0:T(8,128)(2,1)S(1)} %bitcast.36), channel_id=1, source_target_pairs={{0,4},{4,8},{8,12},{12,16},{16,20},{20,24},{24,28},{28,32},{32,36}... | collective-permute-start | bytes 786440 | tf_op jit(solution)/shard_map/ppermute | solution.py:294
  14.8 28.7 %collective-permute-start.3 = (bf16[6,160,256]{2,1,0:T(8,128)(2,1)S(1)}, bf16[6,160,256]{2,1,0:T(8,128)(2,1)S(1)}, u32[]{:S(2)}, u32[]{:S(2)}) collective-permute-start(bf16[6,160,256]{2,1,0:T(8,128)(2,1)S(1)} %slice.16), channel_id=1, source_target_pairs={{4,8},{12,16},{20,24},{28,32},{36,40},{44,48},{52,56},{60,64},{68,... | collective-permute-start | bytes 1474568 | tf_op jit(solution)/shard_map/ppermute | solution.py:297
  16.1 27.4 %collective-permute-start.5 = (bf16[6,96,256]{2,1,0:T(8,128)(2,1)S(1)}, bf16[6,96,256]{2,1,0:T(8,128)(2,1)S(1)}, u32[]{:S(2)}, u32[]{:S(2)}) collective-permute-start(bf16[6,96,256]{2,1,0:T(8,128)(2,1)S(1)} %collective-permute-done.4.piece), channel_id=1, source_target_pairs={{60,256},{316,0},{61,257},{317,1},{62,258},{318,2},{63,259},{319,3}} | collective-permute-start | bytes 884744 | tf_op jit(solution)/shard_map/ppermute | solution.py:299

commit v4 on v3

--- a/solution.py
+++ b/solution.py
@@ -310,7 +310,8 @@
     summand = apply_call(facts, gathered, left_env, right_env)
     parts = lax.all_to_all(summand, "term", 0, 0, tiled=True)
     share, rounded = update(parts, share)
-    gathered = lax.all_gather(rounded, "term")
+    copies = jnp.broadcast_to(rounded, (size, *rounded.shape))
+    gathered = lax.all_to_all(copies, "term", 0, 0, tiled=True)
     return final_call(gathered)
 
 

time: 109 us -> 108 us (level)
  blocking collectives: 59.7 us -> 58 us
    all_gather x2 -> x1, blocking collectives: 29.9 us -> 15.5 us  [shards(): gathered = lax.all_gather(rounded, 'term')]
    all_to_all x0 -> x1, blocking collectives: none -> 12.7 us  [shards(): gathered = lax.all_to_all(copies, 'term', 0, 0, tiled=True)]
where the time goes in v4:
time: 108 us; the launch traced here: 107 us
  blocking collectives  58 us (54%)
  waiting for transfers between devices  22.7 us (21%)
  starting transfers between devices  12.5 us (12%)
  Pallas kernels  11.6 us (11%)
  local copies, waits for them, and re-layouts  1.98 us (2%)
    all_to_all x2, blocking collectives, shards(): parts = lax.all_to_all(summand, 'term', 0, 0, tiled=True)  29.8 us
    ppermute x1, waiting for transfers between devices, shards(): last = lax.ppermute(own_last, 'sec', onward)  15.6 us
    all_gather x1, blocking collectives, shards(): gathered = lax.all_gather(rounded, 'term')  15.5 us
    all_to_all x1, blocking collectives, shards(): gathered = lax.all_to_all(copies, 'term', 0, 0, tiled=True)  12.7 us
    ppermute x1, waiting for transfers between devices, shards(): came = lax.ppermute(fresh[:, :cut], 'sec', odd_on)  7.09 us
    ppermute x1, starting transfers between devices, shards(): last = lax.ppermute(own_last, 'sec', onward)  4.84 us
    pallas_call x1, Pallas kernels, first_call(): call(first_body, [jax.ShapeDtypeStruct((4, terms * bond, bond), BF16), ja...  3.33 us
    pallas_call x2, Pallas kernels, extend_call(): call(body, jax.ShapeDtypeStruct(env.shape, BF16), [SMEM, VMEM, VMEM], [pl...  2.86 us
  transfers between devices with their start and end apart: 6, of which 2 were waited for; matrix products, arithmetic and copies ran while one was open for 0% of the time, Pallas kernels for 4%

profile of v4, /device:TPU:64, one launch (start us, length us, event | category | flops | bytes accessed | tf_op | source)
XLA Modules:
  0.0 107.2 jit_solution(13802136476939913366)
XLA Ops:
  0.0 0.8 slice_bitcast_fusion
  0.8 1.0 copy.17
  1.7 0.1 concatenate.3.facts
  1.8 0.0 copy-start
  1.8 0.0 copy-start.1
  1.8 2.3 %shard_map.55 = bf16[6,256,256]{2,1,0:T(8,128)(2,1)S(1)} custom-call(s32[15]{0:T(128)S(1)} %concatenate.3.facts, bf16[6,256,256]{2,1,0:T(8,128)(2,1)} %bitcast.9.env.own_env, bf16[2,256,256]{2,1,0:T(8,128)(2,1)S(1)} %bitcast.30), custom_call_target="tpu_custom_call" | custom-call | flops 805306368 | bytes 1835008 | tf_op jit(solution)/shard_map/pallas_call | solution.py:88
  4.1 1.9 %collective-permute-start.2 = (bf16[6,256,256]{2,1,0:T(8,128)(2,1)S(1)}, bf16[6,256,256]{2,1,0:T(8,128)(2,1)S(1)}, u32[]{:S(2)}, u32[]{:S(2)}) collective-permute-start(bf16[6,256,256]{2,1,0:T(8,128)(2,1)S(1)} %shard_map.55), channel_id=1, source_target_pairs={{0,4},{4,0},{8,12},{12,8},{16,20},{20,16},{24,28},{28,24},{32,36},... | collective-permute-start | bytes 2359304 | tf_op jit(solution)/shard_map/ppermute | solution.py:292
  6.1 2.5 %collective-permute-start.1 = (bf16[6,256,256]{2,1,0:T(8,128)(2,1)}, bf16[6,256,256]{2,1,0:T(8,128)(2,1)S(1)}, u32[]{:S(2)}, u32[]{:S(2)}) collective-permute-start(bf16[6,256,256]{2,1,0:T(8,128)(2,1)} %bitcast.9.env.own_env), channel_id=1, source_target_pairs={{0,4},{8,12},{16,20},{24,28},{32,36},{40,44},{48,52},{56,60},{64,6... | collective-permute-start | bytes 2359304 | tf_op jit(solution)/shard_map/ppermute | solution.py:293
  8.5 0.0 collective-permute-done.2.once.env
  8.5 0.5 shard_map.57
  9.1 0.7 collective-permute-start.4
  9.8 0.0 copy-done
  9.9 4.8 %collective-permute-start = (bf16[2,256,256]{2,1,0:T(8,128)(2,1)S(1)}, bf16[2,256,256]{2,1,0:T(8,128)(2,1)S(1)}, u32[]{:S(2)}, u32[]{:S(2)}) collective-permute-start(bf16[2,256,256]{2,1,0:T(8,128)(2,1)S(1)} %bitcast.34), channel_id=1, source_target_pairs={{0,4},{4,8},{8,12},{12,16},{16,20},{20,24},{24,28},{28,32},{32,36}... | collective-permute-start | bytes 786440 | tf_op jit(solution)/shard_map/ppermute | solution.py:294
  14.7 0.0 copy-done.1
  14.8 1.3 %collective-permute-start.3 = (bf16[6,160,256]{2,1,0:T(8,128)(2,1)S(1)}, bf16[6,160,256]{2,1,0:T(8,128)(2,1)S(1)}, u32[]{:S(2)}, u32[]{:S(2)}) collective-permute-start(bf16[6,160,256]{2,1,0:T(8,128)(2,1)S(1)} %slice.16), channel_id=1, source_target_pairs={{4,8},{12,16},{20,24},{28,32},{36,40},{44,48},{52,56},{60,64},{68,... | collective-permute-start | bytes 1474568 | tf_op jit(solution)/shard_map/ppermute | solution.py:297
  16.1 0.0 collective-permute-done.4.piece
  16.1 1.3 %collective-permute-start.5 = (bf16[6,96,256]{2,1,0:T(8,128)(2,1)S(1)}, bf16[6,96,256]{2,1,0:T(8,128)(2,1)S(1)}, u32[]{:S(2)}, u32[]{:S(2)}) collective-permute-start(bf16[6,96,256]{2,1,0:T(8,128)(2,1)S(1)} %collective-permute-done.4.piece), channel_id=1, source_target_pairs={{60,256},{316,0},{61,257},{317,1},{62,258},{318,2},{63,259},{319,3}} | collective-permute-start | bytes 884744 | tf_op jit(solution)/shard_map/ppermute | solution.py:299
  17.4 15.6 %collective-permute-done.last = bf16[2,256,256]{2,1,0:T(8,128)(2,1)S(1)} collective-permute-done((bf16[2,256,256]{2,1,0:T(8,128)(2,1)S(1)}, bf16[2,256,256]{2,1,0:T(8,128)(2,1)S(1)}, u32[]{:S(2)}, u32[]{:S(2)}) %collective-permute-start) | collective-permute-done | bytes 262176 | tf_op jit(solution)/shard_map/ppermute | solution.py:294
  33.1 0.0 collective-permute-done.1.partner
  33.1 3.3 %shard_map.56 = (bf16[4,1536,256]{2,1,0:T(8,128)(2,1)S(1)}, f32[4,64,256]{2,1,0:T(8,128)S(1)}, bf16[4,4,64,256]{3,2,1,0:T(8,128)(2,1)S(1)}, bf16[6,256,256]{2,1,0:T(8,128)(2,1)S(1)}) custom-call(s32[15]{0:T(128)S(1)} %concatenate.3.facts, bf16[2,256,256]{2,1,0:T(8,128)(2,1)S(1)} %collective-permute-done.last, bf16[2,256,256]{2,1,0:T(8,128)(2,1)S(1)} %bitcast.33, ...), custom_call_target="tpu_custom_call" | custom-call | flops 67108864000 | tf_op jit(solution)/shard_map/pallas_call | solution.py:151
  36.4 7.1 %collective-permute-done.3.came = bf16[6,160,256]{2,1,0:T(8,128)(2,1)S(1)} collective-permute-done((bf16[6,160,256]{2,1,0:T(8,128)(2,1)S(1)}, bf16[6,160,256]{2,1,0:T(8,128)(2,1)S(1)}, u32[]{:S(2)}, u32[]{:S(2)}) %collective-permute-start.3) | collective-permute-done | bytes 491552 | tf_op jit(solution)/shard_map/ppermute | solution.py:297
  43.5 0.0 collective-permute-done.5.relayed
  43.5 1.5 %shard_map.58 = (bf16[4,4,64,256]{3,2,1,0:T(8,128)(2,1)S(1)}, bf16[6,256,256]{2,1,0:T(8,128)(2,1)S(1)}) custom-call(s32[15]{0:T(128)S(1)} %concatenate.3.facts, bf16[4,1536,256]{2,1,0:T(8,128)(2,1)S(1)} %get-tuple-element.16.applied, bf16[4,4,64,256]{3,2,1,0:T(8,128)(2,1)S(1)} %get-tuple-element.17.before, ...), custom_call_target="tpu_custom_call" | custom-call | flops 805306368 | bytes 5505024 | tf_op jit(solution)/shard_map/pallas_call | solution.py:190
  45.0 16.2 %all_to_all.15 = bf16[4,4,64,256]{3,2,1,0:T(8,128)(2,1)S(1)} all-to-all(bf16[4,4,64,256]{3,2,1,0:T(8,128)(2,1)S(1)} %get-tuple-element.18), channel_id=1, replica_groups=mesh['sec'=128,'term'=4] {'term'}, dimensions={0} | all-to-all | bytes 1048576 | tf_op jit(solution)/shard_map/all_to_all | solution.py:307
  61.3 0.1 convert_reduce_fusion.1
  61.4 15.5 %all-gather = bf16[16,64,256]{2,1,0:T(8,128)(2,1)S(1)} all-gather(bf16[4,64,256]{2,1,0:T(8,128)(2,1)S(1)} %fusion), channel_id=2, replica_groups=mesh['sec'=128,'term'=4] {'term'}, dimensions={0}, use_global_device_ids=true | all-gather | bytes 655360 | tf_op jit(solution)/shard_map/all_gather | solution.py:309
  76.9 2.6 %shard_map.59 = bf16[4,4,64,256]{3,2,1,0:T(8,128)(2,1)S(1)} custom-call(s32[15]{0:T(128)S(1)} %concatenate.3.facts, bf16[4,4,64,256]{3,2,1,0:T(8,128)(2,1)S(1)} %bitcast.29, bf16[6,256,256]{2,1,0:T(8,128)(2,1)S(1)} %get-tuple-element.19.left_env, bf16[6,256,256]{2,1,0:T(8,128)(2,1)S(1)} %get-tuple-element.20.right_env), custom_call_target="tpu_custom_call" | custom-call | flops 1610612736 | bytes 3145728 | tf_op jit(solution)/shard_map/pallas_call | solution.py:215
  79.5 13.5 %all_to_all.16 = bf16[4,4,64,256]{3,2,1,0:T(8,128)(2,1)S(1)} all-to-all(bf16[4,4,64,256]{3,2,1,0:T(8,128)(2,1)S(1)} %shard_map.59), channel_id=1, replica_groups=mesh['sec'=128,'term'=4] {'term'}, dimensions={0} | all-to-all | bytes 1048576 | tf_op jit(solution)/shard_map/all_to_all | solution.py:311
  93.0 0.1 convert_reduce_fusion
  93.1 0.1 subtract_convert_fusion
  93.2 12.7 %all_to_all.17.gathered = bf16[4,4,64,256]{3,2,1,0:T(8,128)(2,1)S(1)} all-to-all(bf16[4,4,64,256]{3,2,1,0:T(8,128)(2,1)S(1)} %broadcast_in_dim.3), channel_id=1, replica_groups=mesh['sec'=128,'term'=4] {'term'}, dimensions={0} | all-to-all | bytes 1048576 | tf_op jit(solution)/shard_map/all_to_all | solution.py:314
  105.9 1.3 %shard_map.60 = f32[2048,128]{1,0:T(8,128)} custom-call(bf16[4,4,64,256]{3,2,1,0:T(8,128)(2,1)S(1)} %all_to_all.17.gathered), custom_call_target="tpu_custom_call" | custom-call | bytes 1572864 | tf_op jit(solution)/shard_map/pallas_call | solution.py:253
  (6 shorter events, 0.2 us)
Async XLA Ops:
  1.8 8.0 %copy-start = (bf16[1,256,2,256]{3,2,1,0:T(2,128)(2,1)S(1)}, bf16[1,256,2,256]{3,2,1,0:T(2,128)(2,1)}, u32[]{:S(2)}) copy-start(bf16[1,256,2,256]{3,2,1,0:T(2,128)(2,1)} %param.7) | copy-start | bytes 786436
  1.8 12.9 %copy-start.1 = (bf16[1,256,2,256]{3,2,1,0:T(2,128)(2,1)S(1)}, bf16[1,256,2,256]{3,2,1,0:T(2,128)(2,1)}, u32[]{:S(2)}) copy-start(bf16[1,256,2,256]{3,2,1,0:T(2,128)(2,1)} %param.8) | copy-start | bytes 786436
  4.1 4.4 %collective-permute-start.2 = (bf16[6,256,256]{2,1,0:T(8,128)(2,1)S(1)}, bf16[6,256,256]{2,1,0:T(8,128)(2,1)S(1)}, u32[]{:S(2)}, u32[]{:S(2)}) collective-permute-start(bf16[6,256,256]{2,1,0:T(8,128)(2,1)S(1)} %shard_map.55), channel_id=1, source_target_pairs={{0,4},{4,0},{8,12},{12,8},{16,20},{20,16},{24,28},{28,24},{32,36},... | collective-permute-start | bytes 2359304 | tf_op jit(solution)/shard_map/ppermute | solution.py:292
  6.1 27.0 %collective-permute-start.1 = (bf16[6,256,256]{2,1,0:T(8,128)(2,1)}, bf16[6,256,256]{2,1,0:T(8,128)(2,1)S(1)}, u32[]{:S(2)}, u32[]{:S(2)}) collective-permute-start(bf16[6,256,256]{2,1,0:T(8,128)(2,1)} %bitcast.9.env.own_env), channel_id=1, source_target_pairs={{0,4},{8,12},{16,20},{24,28},{32,36},{40,44},{48,52},{56,60},{64,6... | collective-permute-start | bytes 2359304 | tf_op jit(solution)/shard_map/ppermute | solution.py:293
  9.1 7.0 %collective-permute-start.4 = (bf16[6,96,256]{2,1,0:T(8,128)(2,1)S(1)}, bf16[6,96,256]{2,1,0:T(8,128)(2,1)S(1)}, u32[]{:S(2)}, u32[]{:S(2)}) collective-permute-start(bf16[6,96,256]{2,1,0:T(8,128)(2,1)S(1)} %slice.17), channel_id=1, source_target_pairs={{4,8},{12,16},{20,24},{28,32},{36,40},{44,48},{52,56},{60,64},{68,... | collective-permute-start | bytes 884744 | tf_op jit(solution)/shard_map/ppermute | solution.py:298
  9.9 23.2 %collective-permute-start = (bf16[2,256,256]{2,1,0:T(8,128)(2,1)S(1)}, bf16[2,256,256]{2,1,0:T(8,128)(2,1)S(1)}, u32[]{:S(2)}, u32[]{:S(2)}) collective-permute-start(bf16[2,256,256]{2,1,0:T(8,128)(2,1)S(1)} %bitcast.34), channel_id=1, source_target_pairs={{0,4},{4,8},{8,12},{12,16},{16,20},{20,24},{24,28},{28,32},{32,36}... | collective-permute-start | bytes 786440 | tf_op jit(solution)/shard_map/ppermute | solution.py:294
  14.8 28.7 %collective-permute-start.3 = (bf16[6,160,256]{2,1,0:T(8,128)(2,1)S(1)}, bf16[6,160,256]{2,1,0:T(8,128)(2,1)S(1)}, u32[]{:S(2)}, u32[]{:S(2)}) collective-permute-start(bf16[6,160,256]{2,1,0:T(8,128)(2,1)S(1)} %slice.16), channel_id=1, source_target_pairs={{4,8},{12,16},{20,24},{28,32},{36,40},{44,48},{52,56},{60,64},{68,... | collective-permute-start | bytes 1474568 | tf_op jit(solution)/shard_map/ppermute | solution.py:297
  16.1 27.4 %collective-permute-start.5 = (bf16[6,96,256]{2,1,0:T(8,128)(2,1)S(1)}, bf16[6,96,256]{2,1,0:T(8,128)(2,1)S(1)}, u32[]{:S(2)}, u32[]{:S(2)}) collective-permute-start(bf16[6,96,256]{2,1,0:T(8,128)(2,1)S(1)} %collective-permute-done.4.piece), channel_id=1, source_target_pairs={{60,256},{316,0},{61,257},{317,1},{62,258},{318,2},{63,259},{319,3}} | collective-permute-start | bytes 884744 | tf_op jit(solution)/shard_map/ppermute | solution.py:299

commit v5 on v4

--- a/solution.py
+++ b/solution.py
@@ -306,7 +306,8 @@
     )
     parts = lax.all_to_all(summand, "term", 0, 0, tiled=True)
     share, rounded = update(parts, share)
-    gathered = lax.all_gather(rounded, "term")
+    copies = jnp.broadcast_to(rounded, (size, *rounded.shape))
+    gathered = lax.all_to_all(copies, "term", 0, 0, tiled=True)
     summand = apply_call(facts, gathered, left_env, right_env)
     parts = lax.all_to_all(summand, "term", 0, 0, tiled=True)
     share, rounded = update(parts, share)

time: 108 us -> 113 us (1.046)
  blocking collectives: 58 us -> 63.2 us
    all_to_all x1 -> x2, blocking collectives: 12.7 us -> 30.9 us  [shards(): gathered = lax.all_to_all(copies, 'term', 0, 0, tiled=True)]
    all_gather x1 -> x0, blocking collectives: 15.5 us -> none  [shards(): gathered = lax.all_gather(rounded, 'term')]
    all_to_all x2, blocking collectives: 29.8 us -> 32.3 us  [shards(): parts = lax.all_to_all(summand, 'term', 0, 0, tiled=True)]
  transfers between devices with their start and end apart: 6 -> 6, of which waited for: 2 -> 2; matrix products, arithmetic and copies ran while one was open for 0% -> 0% of each run, Pallas kernels for 4% -> 3%
where the time goes in v5:
time: 113 us
  blocking collectives  63.2 us (56%)
  waiting for transfers between devices  22.7 us (20%)
  starting transfers between devices  12.5 us (11%)
  Pallas kernels  11.6 us (10%)
  local copies, waits for them, and re-layouts  2.02 us (2%)
    all_to_all x2, blocking collectives, shards(): parts = lax.all_to_all(summand, 'term', 0, 0, tiled=True)  32.3 us
    all_to_all x2, blocking collectives, shards(): gathered = lax.all_to_all(copies, 'term', 0, 0, tiled=True)  30.9 us
    ppermute x1, waiting for transfers between devices, shards(): last = lax.ppermute(own_last, 'sec', onward)  15.6 us
    ppermute x1, waiting for transfers between devices, shards(): came = lax.ppermute(fresh[:, :cut], 'sec', odd_on)  7.09 us
    ppermute x1, starting transfers between devices, shards(): last = lax.ppermute(own_last, 'sec', onward)  4.84 us
    pallas_call x1, Pallas kernels, first_call(): call(first_body, [jax.ShapeDtypeStruct((4, terms * bond, bond), BF16), ja...  3.33 us
    pallas_call x2, Pallas kernels, extend_call(): call(body, jax.ShapeDtypeStruct(env.shape, BF16), [SMEM, VMEM, VMEM], [pl...  2.86 us
    pallas_call x1, Pallas kernels, apply_call(): call(apply_body, jax.ShapeDtypeStruct(gathered.shape, BF16), [SMEM] + [VM...  2.58 us
  transfers between devices with their start and end apart: 6, of which 2 were waited for; matrix products, arithmetic and copies ran while one was open for 0% of the time, Pallas kernels for 3%

profile of v5, /device:TPU:64, one launch (start us, length us, event | category | flops | bytes accessed | tf_op | source)
XLA Modules:
  0.0 112.5 jit_solution(414132537469846570)
XLA Ops:
  0.0 0.8 slice_bitcast_fusion
  0.8 1.0 copy.13
  1.7 0.1 concatenate.3.facts
  1.8 0.0 copy-start
  1.8 0.0 copy-start.1
  1.8 2.3 %shard_map.55 = bf16[6,256,256]{2,1,0:T(8,128)(2,1)S(1)} custom-call(s32[15]{0:T(128)S(1)} %concatenate.3.facts, bf16[6,256,256]{2,1,0:T(8,128)(2,1)} %bitcast.9.env.own_env, bf16[2,256,256]{2,1,0:T(8,128)(2,1)S(1)} %bitcast.28), custom_call_target="tpu_custom_call" | custom-call | flops 805306368 | bytes 1835008 | tf_op jit(solution)/shard_map/pallas_call | solution.py:88
  4.1 1.9 %collective-permute-start.2 = (bf16[6,256,256]{2,1,0:T(8,128)(2,1)S(1)}, bf16[6,256,256]{2,1,0:T(8,128)(2,1)S(1)}, u32[]{:S(2)}, u32[]{:S(2)}) collective-permute-start(bf16[6,256,256]{2,1,0:T(8,128)(2,1)S(1)} %shard_map.55), channel_id=1, source_target_pairs={{0,4},{4,0},{8,12},{12,8},{16,20},{20,16},{24,28},{28,24},{32,36},... | collective-permute-start | bytes 2359304 | tf_op jit(solution)/shard_map/ppermute | solution.py:292
  6.1 2.5 %collective-permute-start.1 = (bf16[6,256,256]{2,1,0:T(8,128)(2,1)}, bf16[6,256,256]{2,1,0:T(8,128)(2,1)S(1)}, u32[]{:S(2)}, u32[]{:S(2)}) collective-permute-start(bf16[6,256,256]{2,1,0:T(8,128)(2,1)} %bitcast.9.env.own_env), channel_id=1, source_target_pairs={{0,4},{8,12},{16,20},{24,28},{32,36},{40,44},{48,52},{56,60},{64,6... | collective-permute-start | bytes 2359304 | tf_op jit(solution)/shard_map/ppermute | solution.py:293
  8.5 0.0 collective-permute-done.2.once.env
  8.5 0.5 shard_map.57
  9.1 0.7 collective-permute-start.4
  9.8 0.0 copy-done
  9.9 4.8 %collective-permute-start = (bf16[2,256,256]{2,1,0:T(8,128)(2,1)S(1)}, bf16[2,256,256]{2,1,0:T(8,128)(2,1)S(1)}, u32[]{:S(2)}, u32[]{:S(2)}) collective-permute-start(bf16[2,256,256]{2,1,0:T(8,128)(2,1)S(1)} %bitcast.32), channel_id=1, source_target_pairs={{0,4},{4,8},{8,12},{12,16},{16,20},{20,24},{24,28},{28,32},{32,36}... | collective-permute-start | bytes 786440 | tf_op jit(solution)/shard_map/ppermute | solution.py:294
  14.7 0.0 copy-done.1
  14.8 1.3 %collective-permute-start.3 = (bf16[6,160,256]{2,1,0:T(8,128)(2,1)S(1)}, bf16[6,160,256]{2,1,0:T(8,128)(2,1)S(1)}, u32[]{:S(2)}, u32[]{:S(2)}) collective-permute-start(bf16[6,160,256]{2,1,0:T(8,128)(2,1)S(1)} %slice.16), channel_id=1, source_target_pairs={{4,8},{12,16},{20,24},{28,32},{36,40},{44,48},{52,56},{60,64},{68,... | collective-permute-start | bytes 1474568 | tf_op jit(solution)/shard_map/ppermute | solution.py:297
  16.1 0.0 collective-permute-done.4.piece
  16.1 1.3 %collective-permute-start.5 = (bf16[6,96,256]{2,1,0:T(8,128)(2,1)S(1)}, bf16[6,96,256]{2,1,0:T(8,128)(2,1)S(1)}, u32[]{:S(2)}, u32[]{:S(2)}) collective-permute-start(bf16[6,96,256]{2,1,0:T(8,128)(2,1)S(1)} %collective-permute-done.4.piece), channel_id=1, source_target_pairs={{60,256},{316,0},{61,257},{317,1},{62,258},{318,2},{63,259},{319,3}} | collective-permute-start | bytes 884744 | tf_op jit(solution)/shard_map/ppermute | solution.py:299
  17.4 15.6 %collective-permute-done.last = bf16[2,256,256]{2,1,0:T(8,128)(2,1)S(1)} collective-permute-done((bf16[2,256,256]{2,1,0:T(8,128)(2,1)S(1)}, bf16[2,256,256]{2,1,0:T(8,128)(2,1)S(1)}, u32[]{:S(2)}, u32[]{:S(2)}) %collective-permute-start) | collective-permute-done | bytes 262176 | tf_op jit(solution)/shard_map/ppermute | solution.py:294
  33.1 0.0 collective-permute-done.1.partner
  33.1 3.3 %shard_map.56 = (bf16[4,1536,256]{2,1,0:T(8,128)(2,1)S(1)}, f32[4,64,256]{2,1,0:T(8,128)S(1)}, bf16[4,4,64,256]{3,2,1,0:T(8,128)(2,1)S(1)}, bf16[6,256,256]{2,1,0:T(8,128)(2,1)S(1)}) custom-call(s32[15]{0:T(128)S(1)} %concatenate.3.facts, bf16[2,256,256]{2,1,0:T(8,128)(2,1)S(1)} %collective-permute-done.last, bf16[2,256,256]{2,1,0:T(8,128)(2,1)S(1)} %bitcast.31, ...), custom_call_target="tpu_custom_call" | custom-call | flops 67108864000 | tf_op jit(solution)/shard_map/pallas_call | solution.py:151
  36.4 7.1 %collective-permute-done.3.came = bf16[6,160,256]{2,1,0:T(8,128)(2,1)S(1)} collective-permute-done((bf16[6,160,256]{2,1,0:T(8,128)(2,1)S(1)}, bf16[6,160,256]{2,1,0:T(8,128)(2,1)S(1)}, u32[]{:S(2)}, u32[]{:S(2)}) %collective-permute-start.3) | collective-permute-done | bytes 491552 | tf_op jit(solution)/shard_map/ppermute | solution.py:297
  43.5 0.0 collective-permute-done.5.relayed
  43.5 1.5 %shard_map.58 = (bf16[4,4,64,256]{3,2,1,0:T(8,128)(2,1)S(1)}, bf16[6,256,256]{2,1,0:T(8,128)(2,1)S(1)}) custom-call(s32[15]{0:T(128)S(1)} %concatenate.3.facts, bf16[4,1536,256]{2,1,0:T(8,128)(2,1)S(1)} %get-tuple-element.16.applied, bf16[4,4,64,256]{3,2,1,0:T(8,128)(2,1)S(1)} %get-tuple-element.17.before, ...), custom_call_target="tpu_custom_call" | custom-call | flops 805306368 | bytes 5505024 | tf_op jit(solution)/shard_map/pallas_call | solution.py:190
  45.0 17.2 %all_to_all.20 = bf16[4,4,64,256]{3,2,1,0:T(8,128)(2,1)S(1)} all-to-all(bf16[4,4,64,256]{3,2,1,0:T(8,128)(2,1)S(1)} %get-tuple-element.18), channel_id=1, replica_groups=mesh['sec'=128,'term'=4] {'term'}, dimensions={0} | all-to-all | bytes 1048576 | tf_op jit(solution)/shard_map/all_to_all | solution.py:307
  62.2 0.1 convert_reduce_fusion.1
  62.4 18.1 %all_to_all.21.gathered = bf16[4,4,64,256]{3,2,1,0:T(8,128)(2,1)S(1)} all-to-all(bf16[4,4,64,256]{3,2,1,0:T(8,128)(2,1)S(1)} %broadcast_in_dim.6), channel_id=1, replica_groups=mesh['sec'=128,'term'=4] {'term'}, dimensions={0} | all-to-all | bytes 1048576 | tf_op jit(solution)/shard_map/all_to_all | solution.py:310
  80.5 2.6 %shard_map.59 = bf16[4,4,64,256]{3,2,1,0:T(8,128)(2,1)S(1)} custom-call(s32[15]{0:T(128)S(1)} %concatenate.3.facts, bf16[4,4,64,256]{3,2,1,0:T(8,128)(2,1)S(1)} %all_to_all.21.gathered, bf16[6,256,256]{2,1,0:T(8,128)(2,1)S(1)} %get-tuple-element.19.left_env, bf16[6,256,256]{2,1,0:T(8,128)(2,1)S(1)} %get-tuple-element.20.right_env), custom_call_target="tpu_custom_call" | custom-call | flops 1610612736 | bytes 3145728 | tf_op jit(solution)/shard_map/pallas_call | solution.py:215
  83.1 15.1 %all_to_all.22 = bf16[4,4,64,256]{3,2,1,0:T(8,128)(2,1)S(1)} all-to-all(bf16[4,4,64,256]{3,2,1,0:T(8,128)(2,1)S(1)} %shard_map.59), channel_id=1, replica_groups=mesh['sec'=128,'term'=4] {'term'}, dimensions={0} | all-to-all | bytes 1048576 | tf_op jit(solution)/shard_map/all_to_all | solution.py:312
  98.2 0.1 convert_reduce_fusion
  98.3 0.1 subtract_convert_fusion
  98.4 12.8 %all_to_all.23.gathered = bf16[4,4,64,256]{3,2,1,0:T(8,128)(2,1)S(1)} all-to-all(bf16[4,4,64,256]{3,2,1,0:T(8,128)(2,1)S(1)} %broadcast_in_dim.7), channel_id=1, replica_groups=mesh['sec'=128,'term'=4] {'term'}, dimensions={0} | all-to-all | bytes 1048576 | tf_op jit(solution)/shard_map/all_to_all | solution.py:315
  111.2 1.3 %shard_map.60 = f32[2048,128]{1,0:T(8,128)} custom-call(bf16[4,4,64,256]{3,2,1,0:T(8,128)(2,1)S(1)} %all_to_all.23.gathered), custom_call_target="tpu_custom_call" | custom-call | bytes 1572864 | tf_op jit(solution)/shard_map/pallas_call | solution.py:253
  (7 shorter events, 0.2 us)
Async XLA Ops:
  1.8 8.0 %copy-start = (bf16[1,256,2,256]{3,2,1,0:T(2,128)(2,1)S(1)}, bf16[1,256,2,256]{3,2,1,0:T(2,128)(2,1)}, u32[]{:S(2)}) copy-start(bf16[1,256,2,256]{3,2,1,0:T(2,128)(2,1)} %param.7) | copy-start | bytes 786436
  1.8 12.9 %copy-start.1 = (bf16[1,256,2,256]{3,2,1,0:T(2,128)(2,1)S(1)}, bf16[1,256,2,256]{3,2,1,0:T(2,128)(2,1)}, u32[]{:S(2)}) copy-start(bf16[1,256,2,256]{3,2,1,0:T(2,128)(2,1)} %param.8) | copy-start | bytes 786436
  4.1 4.4 %collective-permute-start.2 = (bf16[6,256,256]{2,1,0:T(8,128)(2,1)S(1)}, bf16[6,256,256]{2,1,0:T(8,128)(2,1)S(1)}, u32[]{:S(2)}, u32[]{:S(2)}) collective-permute-start(bf16[6,256,256]{2,1,0:T(8,128)(2,1)S(1)} %shard_map.55), channel_id=1, source_target_pairs={{0,4},{4,0},{8,12},{12,8},{16,20},{20,16},{24,28},{28,24},{32,36},... | collective-permute-start | bytes 2359304 | tf_op jit(solution)/shard_map/ppermute | solution.py:292
  6.1 27.0 %collective-permute-start.1 = (bf16[6,256,256]{2,1,0:T(8,128)(2,1)}, bf16[6,256,256]{2,1,0:T(8,128)(2,1)S(1)}, u32[]{:S(2)}, u32[]{:S(2)}) collective-permute-start(bf16[6,256,256]{2,1,0:T(8,128)(2,1)} %bitcast.9.env.own_env), channel_id=1, source_target_pairs={{0,4},{8,12},{16,20},{24,28},{32,36},{40,44},{48,52},{56,60},{64,6... | collective-permute-start | bytes 2359304 | tf_op jit(solution)/shard_map/ppermute | solution.py:293
  9.1 7.0 %collective-permute-start.4 = (bf16[6,96,256]{2,1,0:T(8,128)(2,1)S(1)}, bf16[6,96,256]{2,1,0:T(8,128)(2,1)S(1)}, u32[]{:S(2)}, u32[]{:S(2)}) collective-permute-start(bf16[6,96,256]{2,1,0:T(8,128)(2,1)S(1)} %slice.17), channel_id=1, source_target_pairs={{4,8},{12,16},{20,24},{28,32},{36,40},{44,48},{52,56},{60,64},{68,... | collective-permute-start | bytes 884744 | tf_op jit(solution)/shard_map/ppermute | solution.py:298
  9.9 23.2 %collective-permute-start = (bf16[2,256,256]{2,1,0:T(8,128)(2,1)S(1)}, bf16[2,256,256]{2,1,0:T(8,128)(2,1)S(1)}, u32[]{:S(2)}, u32[]{:S(2)}) collective-permute-start(bf16[2,256,256]{2,1,0:T(8,128)(2,1)S(1)} %bitcast.32), channel_id=1, source_target_pairs={{0,4},{4,8},{8,12},{12,16},{16,20},{20,24},{24,28},{28,32},{32,36}... | collective-permute-start | bytes 786440 | tf_op jit(solution)/shard_map/ppermute | solution.py:294
  14.8 28.7 %collective-permute-start.3 = (bf16[6,160,256]{2,1,0:T(8,128)(2,1)S(1)}, bf16[6,160,256]{2,1,0:T(8,128)(2,1)S(1)}, u32[]{:S(2)}, u32[]{:S(2)}) collective-permute-start(bf16[6,160,256]{2,1,0:T(8,128)(2,1)S(1)} %slice.16), channel_id=1, source_target_pairs={{4,8},{12,16},{20,24},{28,32},{36,40},{44,48},{52,56},{60,64},{68,... | collective-permute-start | bytes 1474568 | tf_op jit(solution)/shard_map/ppermute | solution.py:297
  16.1 27.4 %collective-permute-start.5 = (bf16[6,96,256]{2,1,0:T(8,128)(2,1)S(1)}, bf16[6,96,256]{2,1,0:T(8,128)(2,1)S(1)}, u32[]{:S(2)}, u32[]{:S(2)}) collective-permute-start(bf16[6,96,256]{2,1,0:T(8,128)(2,1)S(1)} %collective-permute-done.4.piece), channel_id=1, source_target_pairs={{60,256},{316,0},{61,257},{317,1},{62,258},{318,2},{63,259},{319,3}} | collective-permute-start | bytes 884744 | tf_op jit(solution)/shard_map/ppermute | solution.py:299

commit v6 on v4

--- a/solution.py
+++ b/solution.py
@@ -14,7 +14,7 @@
 
 FIXED = 3
 ROW = 16
-CUT = 10
+CUT = 9
 
 VMEM = pl.BlockSpec(memory_space=pltpu.VMEM)
 SMEM = pl.BlockSpec(memory_space=pltpu.SMEM)

time: 108 us -> 109 us (level)
  blocking collectives: 58 us -> 60.2 us
    all_to_all x2, blocking collectives: 29.8 us -> 31.8 us  [shards(): parts = lax.all_to_all(summand, 'term', 0, 0, tiled=True)]
where the time goes in v6:
time: 109 us
  blocking collectives  60.2 us (55%)
  waiting for transfers between devices  21.9 us (20%)
  starting transfers between devices  12.5 us (11%)
  Pallas kernels  11.6 us (11%)
  local copies, waits for them, and re-layouts  1.98 us (2%)
    all_to_all x2, blocking collectives, shards(): parts = lax.all_to_all(summand, 'term', 0, 0, tiled=True)  31.8 us
    all_gather x1, blocking collectives, shards(): gathered = lax.all_gather(rounded, 'term')  15.7 us
    ppermute x1, waiting for transfers between devices, shards(): last = lax.ppermute(own_last, 'sec', onward)  15.6 us
    all_to_all x1, blocking collectives, shards(): gathered = lax.all_to_all(copies, 'term', 0, 0, tiled=True)  12.8 us
    ppermute x1, waiting for transfers between devices, shards(): came = lax.ppermute(fresh[:, :cut], 'sec', odd_on)  6.2 us
    ppermute x1, starting transfers between devices, shards(): last = lax.ppermute(own_last, 'sec', onward)  4.84 us
    pallas_call x1, Pallas kernels, first_call(): call(first_body, [jax.ShapeDtypeStruct((4, terms * bond, bond), BF16), ja...  3.33 us
    pallas_call x2, Pallas kernels, extend_call(): call(body, jax.ShapeDtypeStruct(env.shape, BF16), [SMEM, VMEM, VMEM], [pl...  2.86 us
  transfers between devices with their start and end apart: 6, of which 2 were waited for; matrix products, arithmetic and copies ran while one was open for 0% of the time, Pallas kernels for 4%

profile of v6, /device:TPU:64, one launch (start us, length us, event | category | flops | bytes accessed | tf_op | source)
XLA Modules:
  0.0 108.6 jit_solution(15585778067657491117)
XLA Ops:
  0.0 0.8 slice_bitcast_fusion
  0.8 1.0 copy.17
  1.7 0.1 concatenate.3.facts
  1.8 0.0 copy-start
  1.8 0.0 copy-start.1
  1.8 2.3 %shard_map.55 = bf16[6,256,256]{2,1,0:T(8,128)(2,1)S(1)} custom-call(s32[15]{0:T(128)S(1)} %concatenate.3.facts, bf16[6,256,256]{2,1,0:T(8,128)(2,1)} %bitcast.9.env.own_env, bf16[2,256,256]{2,1,0:T(8,128)(2,1)S(1)} %bitcast.30), custom_call_target="tpu_custom_call" | custom-call | flops 805306368 | bytes 1835008 | tf_op jit(solution)/shard_map/pallas_call | solution.py:88
  4.1 1.9 %collective-permute-start.2 = (bf16[6,256,256]{2,1,0:T(8,128)(2,1)S(1)}, bf16[6,256,256]{2,1,0:T(8,128)(2,1)S(1)}, u32[]{:S(2)}, u32[]{:S(2)}) collective-permute-start(bf16[6,256,256]{2,1,0:T(8,128)(2,1)S(1)} %shard_map.55), channel_id=1, source_target_pairs={{0,4},{4,0},{8,12},{12,8},{16,20},{20,16},{24,28},{28,24},{32,36},... | collective-permute-start | bytes 2359304 | tf_op jit(solution)/shard_map/ppermute | solution.py:292
  6.1 2.5 %collective-permute-start.1 = (bf16[6,256,256]{2,1,0:T(8,128)(2,1)}, bf16[6,256,256]{2,1,0:T(8,128)(2,1)S(1)}, u32[]{:S(2)}, u32[]{:S(2)}) collective-permute-start(bf16[6,256,256]{2,1,0:T(8,128)(2,1)} %bitcast.9.env.own_env), channel_id=1, source_target_pairs={{0,4},{8,12},{16,20},{24,28},{32,36},{40,44},{48,52},{56,60},{64,6... | collective-permute-start | bytes 2359304 | tf_op jit(solution)/shard_map/ppermute | solution.py:293
  8.5 0.0 collective-permute-done.2.once.env
  8.5 0.5 shard_map.57
  9.1 0.7 collective-permute-start.4
  9.8 0.0 copy-done
  9.9 4.8 %collective-permute-start = (bf16[2,256,256]{2,1,0:T(8,128)(2,1)S(1)}, bf16[2,256,256]{2,1,0:T(8,128)(2,1)S(1)}, u32[]{:S(2)}, u32[]{:S(2)}) collective-permute-start(bf16[2,256,256]{2,1,0:T(8,128)(2,1)S(1)} %bitcast.34), channel_id=1, source_target_pairs={{0,4},{4,8},{8,12},{12,16},{16,20},{20,24},{24,28},{28,32},{32,36}... | collective-permute-start | bytes 786440 | tf_op jit(solution)/shard_map/ppermute | solution.py:294
  14.7 0.0 copy-done.1
  14.8 1.3 %collective-permute-start.3 = (bf16[6,144,256]{2,1,0:T(8,128)(2,1)S(1)}, bf16[6,144,256]{2,1,0:T(8,128)(2,1)S(1)}, u32[]{:S(2)}, u32[]{:S(2)}) collective-permute-start(bf16[6,144,256]{2,1,0:T(8,128)(2,1)S(1)} %slice.16), channel_id=1, source_target_pairs={{4,8},{12,16},{20,24},{28,32},{36,40},{44,48},{52,56},{60,64},{68,... | collective-permute-start | bytes 1327112 | tf_op jit(solution)/shard_map/ppermute | solution.py:297
  16.1 0.0 collective-permute-done.4.piece
  16.1 1.3 %collective-permute-start.5 = (bf16[6,112,256]{2,1,0:T(8,128)(2,1)S(1)}, bf16[6,112,256]{2,1,0:T(8,128)(2,1)S(1)}, u32[]{:S(2)}, u32[]{:S(2)}) collective-permute-start(bf16[6,112,256]{2,1,0:T(8,128)(2,1)S(1)} %collective-permute-done.4.piece), channel_id=1, source_target_pairs={{60,256},{316,0},{61,257},{317,1},{62,258},{318,2},{63,259},{319,3}} | collective-permute-start | bytes 1032200 | tf_op jit(solution)/shard_map/ppermute | solution.py:299
  17.4 15.6 %collective-permute-done.last = bf16[2,256,256]{2,1,0:T(8,128)(2,1)S(1)} collective-permute-done((bf16[2,256,256]{2,1,0:T(8,128)(2,1)S(1)}, bf16[2,256,256]{2,1,0:T(8,128)(2,1)S(1)}, u32[]{:S(2)}, u32[]{:S(2)}) %collective-permute-start) | collective-permute-done | bytes 262176 | tf_op jit(solution)/shard_map/ppermute | solution.py:294
  33.1 0.0 collective-permute-done.1.partner
  33.1 3.3 %shard_map.56 = (bf16[4,1536,256]{2,1,0:T(8,128)(2,1)S(1)}, f32[4,64,256]{2,1,0:T(8,128)S(1)}, bf16[4,4,64,256]{3,2,1,0:T(8,128)(2,1)S(1)}, bf16[6,256,256]{2,1,0:T(8,128)(2,1)S(1)}) custom-call(s32[15]{0:T(128)S(1)} %concatenate.3.facts, bf16[2,256,256]{2,1,0:T(8,128)(2,1)S(1)} %collective-permute-done.last, bf16[2,256,256]{2,1,0:T(8,128)(2,1)S(1)} %bitcast.33, ...), custom_call_target="tpu_custom_call" | custom-call | flops 67108864000 | tf_op jit(solution)/shard_map/pallas_call | solution.py:151
  36.4 6.2 %collective-permute-done.3.came = bf16[6,144,256]{2,1,0:T(8,128)(2,1)S(1)} collective-permute-done((bf16[6,144,256]{2,1,0:T(8,128)(2,1)S(1)}, bf16[6,144,256]{2,1,0:T(8,128)(2,1)S(1)}, u32[]{:S(2)}, u32[]{:S(2)}) %collective-permute-start.3) | collective-permute-done | bytes 442400 | tf_op jit(solution)/shard_map/ppermute | solution.py:297
  42.6 0.0 collective-permute-done.5.relayed
  42.6 1.5 %shard_map.58 = (bf16[4,4,64,256]{3,2,1,0:T(8,128)(2,1)S(1)}, bf16[6,256,256]{2,1,0:T(8,128)(2,1)S(1)}) custom-call(s32[15]{0:T(128)S(1)} %concatenate.3.facts, bf16[4,1536,256]{2,1,0:T(8,128)(2,1)S(1)} %get-tuple-element.16.applied, bf16[4,4,64,256]{3,2,1,0:T(8,128)(2,1)S(1)} %get-tuple-element.17.before, ...), custom_call_target="tpu_custom_call" | custom-call | flops 805306368 | bytes 5505024 | tf_op jit(solution)/shard_map/pallas_call | solution.py:190
  44.1 17.2 %all_to_all.15 = bf16[4,4,64,256]{3,2,1,0:T(8,128)(2,1)S(1)} all-to-all(bf16[4,4,64,256]{3,2,1,0:T(8,128)(2,1)S(1)} %get-tuple-element.18), channel_id=1, replica_groups=mesh['sec'=128,'term'=4] {'term'}, dimensions={0} | all-to-all | bytes 1048576 | tf_op jit(solution)/shard_map/all_to_all | solution.py:307
  61.3 0.1 convert_reduce_fusion.1
  61.4 15.7 %all-gather = bf16[16,64,256]{2,1,0:T(8,128)(2,1)S(1)} all-gather(bf16[4,64,256]{2,1,0:T(8,128)(2,1)S(1)} %fusion), channel_id=2, replica_groups=mesh['sec'=128,'term'=4] {'term'}, dimensions={0}, use_global_device_ids=true | all-gather | bytes 655360 | tf_op jit(solution)/shard_map/all_gather | solution.py:309
  77.1 2.6 %shard_map.59 = bf16[4,4,64,256]{3,2,1,0:T(8,128)(2,1)S(1)} custom-call(s32[15]{0:T(128)S(1)} %concatenate.3.facts, bf16[4,4,64,256]{3,2,1,0:T(8,128)(2,1)S(1)} %bitcast.29, bf16[6,256,256]{2,1,0:T(8,128)(2,1)S(1)} %get-tuple-element.19.left_env, bf16[6,256,256]{2,1,0:T(8,128)(2,1)S(1)} %get-tuple-element.20.right_env), custom_call_target="tpu_custom_call" | custom-call | flops 1610612736 | bytes 3145728 | tf_op jit(solution)/shard_map/pallas_call | solution.py:215
  79.7 14.6 %all_to_all.16 = bf16[4,4,64,256]{3,2,1,0:T(8,128)(2,1)S(1)} all-to-all(bf16[4,4,64,256]{3,2,1,0:T(8,128)(2,1)S(1)} %shard_map.59), channel_id=1, replica_groups=mesh['sec'=128,'term'=4] {'term'}, dimensions={0} | all-to-all | bytes 1048576 | tf_op jit(solution)/shard_map/all_to_all | solution.py:311
  94.3 0.1 convert_reduce_fusion
  94.4 0.1 subtract_convert_fusion
  94.5 12.8 %all_to_all.17.gathered = bf16[4,4,64,256]{3,2,1,0:T(8,128)(2,1)S(1)} all-to-all(bf16[4,4,64,256]{3,2,1,0:T(8,128)(2,1)S(1)} %broadcast_in_dim.3), channel_id=1, replica_groups=mesh['sec'=128,'term'=4] {'term'}, dimensions={0} | all-to-all | bytes 1048576 | tf_op jit(solution)/shard_map/all_to_all | solution.py:314
  107.3 1.3 %shard_map.60 = f32[2048,128]{1,0:T(8,128)} custom-call(bf16[4,4,64,256]{3,2,1,0:T(8,128)(2,1)S(1)} %all_to_all.17.gathered), custom_call_target="tpu_custom_call" | custom-call | bytes 1572864 | tf_op jit(solution)/shard_map/pallas_call | solution.py:253
  (6 shorter events, 0.2 us)
Async XLA Ops:
  1.8 8.0 %copy-start = (bf16[1,256,2,256]{3,2,1,0:T(2,128)(2,1)S(1)}, bf16[1,256,2,256]{3,2,1,0:T(2,128)(2,1)}, u32[]{:S(2)}) copy-start(bf16[1,256,2,256]{3,2,1,0:T(2,128)(2,1)} %param.7) | copy-start | bytes 786436
  1.8 12.9 %copy-start.1 = (bf16[1,256,2,256]{3,2,1,0:T(2,128)(2,1)S(1)}, bf16[1,256,2,256]{3,2,1,0:T(2,128)(2,1)}, u32[]{:S(2)}) copy-start(bf16[1,256,2,256]{3,2,1,0:T(2,128)(2,1)} %param.8) | copy-start | bytes 786436
  4.1 4.4 %collective-permute-start.2 = (bf16[6,256,256]{2,1,0:T(8,128)(2,1)S(1)}, bf16[6,256,256]{2,1,0:T(8,128)(2,1)S(1)}, u32[]{:S(2)}, u32[]{:S(2)}) collective-permute-start(bf16[6,256,256]{2,1,0:T(8,128)(2,1)S(1)} %shard_map.55), channel_id=1, source_target_pairs={{0,4},{4,0},{8,12},{12,8},{16,20},{20,16},{24,28},{28,24},{32,36},... | collective-permute-start | bytes 2359304 | tf_op jit(solution)/shard_map/ppermute | solution.py:292
  6.1 27.0 %collective-permute-start.1 = (bf16[6,256,256]{2,1,0:T(8,128)(2,1)}, bf16[6,256,256]{2,1,0:T(8,128)(2,1)S(1)}, u32[]{:S(2)}, u32[]{:S(2)}) collective-permute-start(bf16[6,256,256]{2,1,0:T(8,128)(2,1)} %bitcast.9.env.own_env), channel_id=1, source_target_pairs={{0,4},{8,12},{16,20},{24,28},{32,36},{40,44},{48,52},{56,60},{64,6... | collective-permute-start | bytes 2359304 | tf_op jit(solution)/shard_map/ppermute | solution.py:293
  9.1 7.0 %collective-permute-start.4 = (bf16[6,112,256]{2,1,0:T(8,128)(2,1)S(1)}, bf16[6,112,256]{2,1,0:T(8,128)(2,1)S(1)}, u32[]{:S(2)}, u32[]{:S(2)}) collective-permute-start(bf16[6,112,256]{2,1,0:T(8,128)(2,1)S(1)} %slice.17), channel_id=1, source_target_pairs={{4,8},{12,16},{20,24},{28,32},{36,40},{44,48},{52,56},{60,64},{68,... | collective-permute-start | bytes 1032200 | tf_op jit(solution)/shard_map/ppermute | solution.py:298
  9.9 23.2 %collective-permute-start = (bf16[2,256,256]{2,1,0:T(8,128)(2,1)S(1)}, bf16[2,256,256]{2,1,0:T(8,128)(2,1)S(1)}, u32[]{:S(2)}, u32[]{:S(2)}) collective-permute-start(bf16[2,256,256]{2,1,0:T(8,128)(2,1)S(1)} %bitcast.34), channel_id=1, source_target_pairs={{0,4},{4,8},{8,12},{12,16},{16,20},{20,24},{24,28},{28,32},{32,36}... | collective-permute-start | bytes 786440 | tf_op jit(solution)/shard_map/ppermute | solution.py:294
  14.8 27.8 %collective-permute-start.3 = (bf16[6,144,256]{2,1,0:T(8,128)(2,1)S(1)}, bf16[6,144,256]{2,1,0:T(8,128)(2,1)S(1)}, u32[]{:S(2)}, u32[]{:S(2)}) collective-permute-start(bf16[6,144,256]{2,1,0:T(8,128)(2,1)S(1)} %slice.16), channel_id=1, source_target_pairs={{4,8},{12,16},{20,24},{28,32},{36,40},{44,48},{52,56},{60,64},{68,... | collective-permute-start | bytes 1327112 | tf_op jit(solution)/shard_map/ppermute | solution.py:297
  16.1 26.5 %collective-permute-start.5 = (bf16[6,112,256]{2,1,0:T(8,128)(2,1)S(1)}, bf16[6,112,256]{2,1,0:T(8,128)(2,1)S(1)}, u32[]{:S(2)}, u32[]{:S(2)}) collective-permute-start(bf16[6,112,256]{2,1,0:T(8,128)(2,1)S(1)} %collective-permute-done.4.piece), channel_id=1, source_target_pairs={{60,256},{316,0},{61,257},{317,1},{62,258},{318,2},{63,259},{319,3}} | collective-permute-start | bytes 1032200 | tf_op jit(solution)/shard_map/ppermute | solution.py:299
